TPU v7x, 32 devices: a whole 2x2x4 slice. The times are simulated.
32 devices in a mesh: groups: 2 (over y), pool: 4 (over x, core), tp: 4 (over z).
Axes of the slice: x: 2, y: 2, z: 4, core: 2. Of those that a mesh axis runs over, the one named last changes fastest.
Arguments:
- inputs: bfloat16 [4, 1024, 8192], P(None, ('groups', 'pool'), 'tp'), parts along dimension 1, may hold values from -6 to 6
- out_weight: bfloat16 [8192, 8192], P('tp'), may hold values from -0.0625 to 0.0625
- shrink_store: bfloat16 [128, 64, 8192], P(('groups', 'pool'), None, 'tp'), parts along dimension 0, may hold values from -0.0625 to 0.0625
- expand_store: bfloat16 [128, 64, 8192], P(('groups', 'pool'), None, 'tp'), parts along dimension 0, may hold values from -0.75 to 0.75
- owner_map: int32 [128], P('groups'), parts along dimension 0, may hold values from 0 to 63, as said below
- requests: int32 [4, 8, 8], P(None, ('groups', 'pool')), parts along dimension 1, may hold values from 0 to 63, as said below
- row_slot: int32 [4, 1024], P(None, ('groups', 'pool')), parts along dimension 1, may hold values from 0 to 7
Outputs:
- projected: bfloat16 [4, 1024, 8192], P(None, ('groups', 'pool'), 'tp'), parts along dimension 1
There are 2 independent parts, one for each index of `groups`. A program takes and returns all parts, laid end to end along the dimension named above; an argument that names none is the same for every part. Nothing has to cross between parts.
Inputs may be any that keep to these rules, and one draw needn't show every extreme that they name: `owner_map`: A permutation: each adapter id has its own store position; position q is held by pool index q // 16. `requests`: each list names 8 distinct adapter ids; at most 2 of them are stored on one pool index, and exactly 2 on some pool index in every list.
All inputs are finite; a program needn't handle non-finite values.
Results may differ from a plain program's by a relative error of at most 0.0047.
Values may be sent and summed in bfloat16 or wider, within the bound.
A program may use at most 192 MiB of HBM per device.

v0:
```python
import jax
import jax.numpy as jnp
from jax import lax
from jax.sharding import PartitionSpec as P

CAP = 2


adapter_scale = 2.0


def owner_ranks(owners):
    count = owners.shape[-1]
    same = owners[..., :, None] == owners[..., None, :]
    earlier = jnp.arange(count)[:, None] < jnp.arange(count)[None, :]
    return jnp.sum((same & earlier).astype(jnp.int32), axis=-2)


def base_term_maker(rows_input, out_weight):

    def term(start, count):
        return lax.dot_general(
            out_weight, rows_input, (((0,), (1,)), ((), ())), preferred_element_type=jnp.float32
        )

    return term


def body(inputs, out_weight, shrink_store, expand_store, owner_map, requests, row_slot):
    steps_count, rows_count, feature_shard = inputs.shape
    stored = shrink_store.shape[0]
    rank_size = shrink_store.shape[1]
    slot_count = requests.shape[2]
    pool_size = lax.axis_size("pool")
    my_index = lax.axis_index("pool")
    adapter_range = jnp.arange(owner_map.shape[0], dtype=jnp.int32)
    shard_rows = out_weight.shape[0]
    own_ids = requests[:, 0, :]
    token_positions = jnp.sum(
        jnp.where(own_ids[:, :, None] == adapter_range[None, None, :], owner_map[None, None, :], 0),
        axis=-1,
    )
    every_position = lax.all_gather(token_positions[None], "pool", axis=0, tiled=True)
    every_owner = every_position // stored
    every_rank = owner_ranks(every_owner)
    every_local = every_position % stored
    capacity_range = jnp.arange(CAP, dtype=jnp.int32)
    matches = (every_owner[:, :, None, :] == my_index) & (
        every_rank[:, :, None, :] == capacity_range[None, None, :, None]
    )
    send_index = jnp.sum(jnp.where(matches, every_local[:, :, None, :], 0), axis=-1)
    send_valid = jnp.any(matches, axis=-1).astype(jnp.bfloat16)[..., None, None]
    send_shrink = shrink_store[send_index] * send_valid
    send_expand = expand_store[send_index] * send_valid
    self_owner_rank = token_positions // stored
    own_flat = self_owner_rank * CAP + owner_ranks(self_owner_rank)
    slot_range = jnp.arange(slot_count, dtype=jnp.int32)
    output_rows = []
    for step_index in range(steps_count):
        recv_shrink, recv_expand = (
            lax.all_to_all(
                send_shrink[:, step_index], "pool", split_axis=0, concat_axis=0, tiled=True
            ),
            lax.all_to_all(
                send_expand[:, step_index], "pool", split_axis=0, concat_axis=0, tiled=True
            ),
        )
        shrink_all = recv_shrink.reshape(pool_size * CAP, rank_size, feature_shard)[
            own_flat[step_index]
        ]
        expand_all = recv_expand.reshape(pool_size * CAP, rank_size, feature_shard)[
            own_flat[step_index]
        ]
        rows_input = inputs[step_index]
        codes = lax.dot_general(
            rows_input,
            shrink_all.reshape(slot_count * rank_size, feature_shard),
            (((1,), (1,)), ((), ())),
            preferred_element_type=jnp.float32,
        )
        onehot = (row_slot[step_index][:, None] == slot_range[None, :]).astype(jnp.float32)
        chosen = jnp.sum(
            codes.reshape(rows_count, slot_count, rank_size) * onehot[:, :, None], axis=1
        )
        code_total = lax.psum(chosen, "tp").astype(jnp.bfloat16)
        spread = (onehot.astype(jnp.bfloat16)[:, :, None] * code_total[:, None, :]).reshape(
            rows_count, slot_count * rank_size
        )
        adapter_delta = jnp.dot(
            spread,
            expand_all.reshape(slot_count * rank_size, feature_shard),
            preferred_element_type=jnp.float32,
        )
        step_term = base_term_maker(rows_input, out_weight)
        frozen_base_share = lax.psum_scatter(
            step_term(jnp.int32(0), lax.axis_size("tp") * shard_rows),
            "tp",
            scatter_dimension=0,
            tiled=True,
        ).T
        output_rows.append((frozen_base_share + adapter_scale * adapter_delta).astype(jnp.bfloat16))
    return jnp.stack(output_rows, axis=0)


def solution(mesh):
    placed = (
        P(None, ("groups", "pool"), "tp"),
        P("tp", None),
        P(("groups", "pool"), None, "tp"),
        P(("groups", "pool"), None, "tp"),
        P("groups"),
        P(None, ("groups", "pool"), None),
        P(None, ("groups", "pool")),
    )
    return jax.shard_map(
        body,
        mesh=mesh,
        in_specs=placed,
        out_specs=P(None, ("groups", "pool"), "tp"),
        check_vma=False,
    )
```

profile of v0, /device:TPU:0, one launch (start us, length us, event | category | flops | bytes accessed | tf_op | source)
XLA Modules:
  0.0 381.4 jit_solution(14253079727512748180)
XLA Ops:
  6.5 16.7 %fusion.30 = f32[8192,128]{1,0:T(8,128)} fusion(bf16[2048,8192]{1,0:T(8,128)(2,1)} %param.8, bf16[4,128,2048]{2,1,0:T(8,128)(2,1)} %param.7), kind=kOutput, calls=%fused_computation.55 | convolution fusion | flops 4294967296 | bytes 38273024 | tf_op jit(solution)/shard_map/dot_general | solution.py:22
  24.8 17.8 %fusion.26 = f32[8192,128]{1,0:T(8,128)} fusion(bf16[2048,8192]{1,0:T(8,128)(2,1)} %param.8, bf16[4,128,2048]{2,1,0:T(8,128)(2,1)S(1)} %copy-done.8), kind=kOutput, calls=%fused_computation.51 | convolution fusion | flops 4294967296 | bytes 38273024 | tf_op jit(solution)/shard_map/dot_general | solution.py:22
  42.9 17.3 %fusion.22 = f32[8192,128]{1,0:T(8,128)} fusion(bf16[2048,8192]{1,0:T(8,128)(2,1)} %param.8, bf16[4,128,2048]{2,1,0:T(8,128)(2,1)S(1)} %copy-done.8), kind=kOutput, calls=%fused_computation.47 | convolution fusion | flops 4294967296 | bytes 38273024 | tf_op jit(solution)/shard_map/dot_general | solution.py:22
  61.0 6.1 %all-gather.1 = s32[4,4,8]{2,1,0:T(4,128)S(1)} all-gather(s32[1,4,8]{2,1,0:T(4,128)S(1)} %bitcast.174), channel_id=2, replica_groups=mesh['groups'=2,'pool'=4,'tp'=4] {'pool'}, dimensions={0}, use_global_device_ids=true | all-gather | bytes 640 | tf_op jit(solution)/shard_map/all_gather | solution.py:43
  68.0 7.2 %gather_fusion.2 = bf16[32,64,2048]{2,1,0:T(8,128)(2,1)} fusion(bf16[16,64,2048]{2,1,0:T(8,128)(2,1)} %param.10, s32[1024]{0:T(1024)S(1)} %pad_clamp_fusion.4), kind=kCustom, calls=%fused_computation.2 | custom fusion | bytes 16777344 | tf_op jit(solution)/shard_map/gather | solution.py:54
  75.2 7.2 %gather_fusion = bf16[32,64,2048]{2,1,0:T(8,128)(2,1)} fusion(bf16[16,64,2048]{2,1,0:T(8,128)(2,1)} %param.9, s32[1024]{0:T(1024)S(1)} %pad_clamp_fusion.4), kind=kCustom, calls=%fused_computation | custom fusion | bytes 16777344 | tf_op jit(solution)/shard_map/gather | solution.py:53
  82.5 9.2 %broadcast_multiply_fusion.1 = (bf16[4,4,2,64,2048]{4,3,2,1,0:T(8,128)(2,1)S(1)}, bf16[4,4,2,64,2048]{4,3,2,1,0:T(8,128)(2,1)}) fusion(bf16[4,4,2,64,2048]{4,3,2,1,0:T(8,128)(2,1)} %bitcast.161, bf16[4,4,2]{2,1,0:T(4,128)(2,1)S(1)} %copy.28, bf16[4,4,2,64,2048]{4,3,2,1,0:T(8,128)(2,1)} %bitcast.160), kind=kLoop, calls=%fused_computation.11 | loop fusion | flops 8388608 | bytes 33554496 | tf_op jit(solution)/shard_map/mul | solution.py:53
  93.8 29.1 %all_to_all.40 = bf16[4,2,64,2048]{3,2,1,0:T(8,128)(2,1)} all-to-all(bf16[4,2,64,2048]{3,2,1,0:T(8,128)(2,1)S(1)} %get-tuple-element.15), channel_id=1, replica_groups=mesh['groups'=2,'pool'=4,'tp'=4] {'pool'}, dimensions={0} | all-to-all | bytes 4194304 | tf_op jit(solution)/shard_map/all_to_all | solution.py:61
  122.9 28.9 %all_to_all.41 = bf16[4,2,64,2048]{3,2,1,0:T(8,128)(2,1)} all-to-all(bf16[4,2,64,2048]{3,2,1,0:T(8,128)(2,1)S(1)} %get-tuple-element.18), channel_id=1, replica_groups=mesh['groups'=2,'pool'=4,'tp'=4] {'pool'}, dimensions={0} | all-to-all | bytes 4194304 | tf_op jit(solution)/shard_map/all_to_all | solution.py:61
  151.8 28.2 %all_to_all.42 = bf16[4,2,64,2048]{3,2,1,0:T(8,128)(2,1)S(1)} all-to-all(bf16[4,2,64,2048]{3,2,1,0:T(8,128)(2,1)S(1)} %get-tuple-element.17), channel_id=1, replica_groups=mesh['groups'=2,'pool'=4,'tp'=4] {'pool'}, dimensions={0} | all-to-all | bytes 4194304 | tf_op jit(solution)/shard_map/all_to_all | solution.py:61
  180.0 4.5 %all-to-all-start.6 = ((bf16[4,2,64,2048]{3,2,1,0:T(8,128)(2,1)}), bf16[4,2,64,2048]{3,2,1,0:T(8,128)(2,1)}, u32[]{:S(2)}, u32[]{:S(2)}) async-start(bf16[4,2,64,2048]{3,2,1,0:T(8,128)(2,1)} %get-tuple-element.16), calls=%async_computation.10 | async-start | bytes 4194304 | tf_op jit(solution)/shard_map/all_to_all | solution.py:61
  184.8 17.5 %fusion.18 = f32[8192,128]{1,0:T(8,128)} fusion(bf16[2048,8192]{1,0:T(8,128)(2,1)} %param.8, bf16[4,128,2048]{2,1,0:T(8,128)(2,1)} %param.7), kind=kOutput, calls=%fused_computation.43 | convolution fusion | flops 4294967296 | bytes 38273024 | tf_op jit(solution)/shard_map/dot_general | solution.py:22
  202.3 6.0 %slice_bitcast_fusion.6 = (bf16[4,2,64,2048]{3,2,1,0:T(8,128)(2,1)}, bf16[4,2,64,2048]{3,2,1,0:T(8,128)(2,1)}, bf16[4,2,64,2048]{3,2,1,0:T(8,128)(2,1)}, bf16[4,2,64,2048]{3,2,1,0:T(8,128)(2,1)}) fusion(bf16[4,4,2,64,2048]{4,3,2,1,0:T(8,128)(2,1)} %get-tuple-element.20), kind=kLoop, calls=%fused_computation.38 | loop fusion | bytes 16777216 | tf_op jit(solution)/shard_map/squeeze | solution.py:65
  210.3 30.1 %all_to_all.43 = bf16[4,2,64,2048]{3,2,1,0:T(8,128)(2,1)} all-to-all(bf16[4,2,64,2048]{3,2,1,0:T(8,128)(2,1)} %get-tuple-element.11), channel_id=1, replica_groups=mesh['groups'=2,'pool'=4,'tp'=4] {'pool'}, dimensions={0} | all-to-all | bytes 4194304 | tf_op jit(solution)/shard_map/all_to_all | solution.py:64
  240.4 4.4 %all-to-all-start.3 = ((bf16[4,2,64,2048]{3,2,1,0:T(8,128)(2,1)}), bf16[4,2,64,2048]{3,2,1,0:T(8,128)(2,1)}, u32[]{:S(2)}, u32[]{:S(2)}) async-start(bf16[4,2,64,2048]{3,2,1,0:T(8,128)(2,1)} %get-tuple-element.14), calls=%async_computation.5 | async-start | bytes 4194304 | tf_op jit(solution)/shard_map/all_to_all | solution.py:64
  245.0 25.7 %all-to-all-done.3 = bf16[4,2,64,2048]{3,2,1,0:T(8,128)(2,1)} async-done(((bf16[4,2,64,2048]{3,2,1,0:T(8,128)(2,1)}), bf16[4,2,64,2048]{3,2,1,0:T(8,128)(2,1)}, u32[]{:S(2)}, u32[]{:S(2)}) %all-to-all-start.3) | async-done | bytes 2097184 | tf_op jit(solution)/shard_map/all_to_all | solution.py:64
  270.6 4.6 %all-to-all-start.5 = ((bf16[4,2,64,2048]{3,2,1,0:T(8,128)(2,1)}), bf16[4,2,64,2048]{3,2,1,0:T(8,128)(2,1)}, u32[]{:S(2)}, u32[]{:S(2)}) async-start(bf16[4,2,64,2048]{3,2,1,0:T(8,128)(2,1)} %get-tuple-element.13), calls=%async_computation.8 | async-start | bytes 4194304 | tf_op jit(solution)/shard_map/all_to_all | solution.py:64
  275.3 25.6 %all-to-all-done.5 = bf16[4,2,64,2048]{3,2,1,0:T(8,128)(2,1)} async-done(((bf16[4,2,64,2048]{3,2,1,0:T(8,128)(2,1)}), bf16[4,2,64,2048]{3,2,1,0:T(8,128)(2,1)}, u32[]{:S(2)}, u32[]{:S(2)}) %all-to-all-start.5) | async-done | bytes 2097184 | tf_op jit(solution)/shard_map/all_to_all | solution.py:64
  301.0 4.4 %all-to-all-start.7 = ((bf16[4,2,64,2048]{3,2,1,0:T(8,128)(2,1)}), bf16[4,2,64,2048]{3,2,1,0:T(8,128)(2,1)}, u32[]{:S(2)}, u32[]{:S(2)}) async-start(bf16[4,2,64,2048]{3,2,1,0:T(8,128)(2,1)} %get-tuple-element.12), calls=%async_computation.11 | async-start | bytes 4194304 | tf_op jit(solution)/shard_map/all_to_all | solution.py:64
  305.4 3.6 gather_fusion.1
  309.1 3.6 gather_fusion.4
  312.6 2.5 fusion.28
  319.0 3.7 gather_fusion.8
  328.7 3.6 gather_fusion.5
  332.2 3.6 gather_fusion.7
  335.8 2.3 gather_fusion.9
  338.1 22.3 %all-reduce.2 = (bf16[128,64]{0,1:T(8,128)(2,1)S(1)}, bf16[128,64]{0,1:T(8,128)(2,1)S(1)}, bf16[128,64]{0,1:T(8,128)(2,1)S(1)}, bf16[128,64]{0,1:T(8,128)(2,1)S(1)}) all-reduce(f32[128,64]{0,1:T(8,128)S(1)} %get-tuple-element.37, f32[128,64]{0,1:T(8,128)S(1)} %get-tuple-element.38, ...), channel_id=1, replica_groups=mesh['groups'=2,'pool'=4,'tp'=4] {'tp'}, use_global_device_ids=true, to_apply=%region_16.17 | all-reduce | flops 32768 | bytes 196608 | tf_op jit(solution)/shard_map/psum | solution.py:85
  360.5 2.8 fusion.15
  363.3 2.8 fusion.14
  366.1 3.6 fusion.13
  369.7 2.2 fusion.12
  372.2 2.6 copy.33
  (67 shorter events, 18.1 us)
Async XLA Ops:
  6.5 353.9 %reduce-scatter.5.cloned.1.call-start = ((), (), s32[]{:S(2)}) async-start(), calls=%async_computation.12 | async-start | bytes 5242880 | tf_op jit(solution)/shard_map/reduce_scatter | solution.py:95
  23.2 1.6 copy-start.8
  23.2 340.1 %reduce-scatter.7.cloned.1.call-start = ((), (), s32[]{:S(2)}) async-start(), calls=%async_computation.13 | async-start | bytes 5242880 | tf_op jit(solution)/shard_map/reduce_scatter | solution.py:95
  42.7 323.5 %reduce-scatter.9.cloned.1.call-start = ((), (), s32[]{:S(2)}) async-start(), calls=%async_computation.14 | async-start | bytes 5242880 | tf_op jit(solution)/shard_map/reduce_scatter | solution.py:95
  60.2 0.7 copy-start.5
  60.2 0.7 copy-start.7
  180.0 30.3 %all-to-all-start.6 = ((bf16[4,2,64,2048]{3,2,1,0:T(8,128)(2,1)}), bf16[4,2,64,2048]{3,2,1,0:T(8,128)(2,1)}, u32[]{:S(2)}, u32[]{:S(2)}) async-start(bf16[4,2,64,2048]{3,2,1,0:T(8,128)(2,1)} %get-tuple-element.16), calls=%async_computation.10 | async-start | bytes 4194304 | tf_op jit(solution)/shard_map/all_to_all | solution.py:61
  184.5 185.2 %reduce-scatter.11.cloned.1.call-start = ((), (), s32[]{:S(2)}) async-start(), calls=%async_computation.15 | async-start | bytes 5242880 | tf_op jit(solution)/shard_map/reduce_scatter | solution.py:95
  240.4 30.2 %all-to-all-start.3 = ((bf16[4,2,64,2048]{3,2,1,0:T(8,128)(2,1)}), bf16[4,2,64,2048]{3,2,1,0:T(8,128)(2,1)}, u32[]{:S(2)}, u32[]{:S(2)}) async-start(bf16[4,2,64,2048]{3,2,1,0:T(8,128)(2,1)} %get-tuple-element.14), calls=%async_computation.5 | async-start | bytes 4194304 | tf_op jit(solution)/shard_map/all_to_all | solution.py:64
  270.6 4.7 %copy-start.6 = (s32[4,128]{1,0:T(4,128)S(1)}, s32[4,128]{1,0:T(4,128)}, u32[]{:S(2)}) copy-start(s32[4,128]{1,0:T(4,128)} %param.13) | copy-start | bytes 6148
  270.6 30.4 %all-to-all-start.5 = ((bf16[4,2,64,2048]{3,2,1,0:T(8,128)(2,1)}), bf16[4,2,64,2048]{3,2,1,0:T(8,128)(2,1)}, u32[]{:S(2)}, u32[]{:S(2)}) async-start(bf16[4,2,64,2048]{3,2,1,0:T(8,128)(2,1)} %get-tuple-element.13), calls=%async_computation.8 | async-start | bytes 4194304 | tf_op jit(solution)/shard_map/all_to_all | solution.py:64
  301.0 34.9 %all-to-all-start.7 = ((bf16[4,2,64,2048]{3,2,1,0:T(8,128)(2,1)}), bf16[4,2,64,2048]{3,2,1,0:T(8,128)(2,1)}, u32[]{:S(2)}, u32[]{:S(2)}) async-start(bf16[4,2,64,2048]{3,2,1,0:T(8,128)(2,1)} %get-tuple-element.12), calls=%async_computation.11 | async-start | bytes 4194304 | tf_op jit(solution)/shard_map/all_to_all | solution.py:64
  312.6 2.5 copy-start.1
  319.0 3.7 copy-start.2
  322.7 1.9 copy-start.3
  324.7 2.0 copy-start
  369.7 2.2 copy-start.4
Sparse Core Ops, SparseCore 0:
  23.3 79.4 reduce-scatter.4
  105.2 77.2 reduce-scatter.6
  184.8 77.2 reduce-scatter.8
  264.4 77.2 reduce-scatter.10
where the time goes:
time: 382 us; the launch traced here: 381 us
  blocking collectives  145 us (38%)
  matrix products  88.8 us (23%)
  waiting for transfers between devices  53.3 us (14%)
  local copies, waits for them, and re-layouts  52 us (14%)
  starting transfers between devices  18.5 us (5%)
  between operations  13.4 us (4%)
  other arithmetic  10.5 us (3%)
    all_to_all x3, blocking collectives, body(): lax.all_to_all(send_shrink[:, step_index], 'pool', split_axis=0, concat_a...  86.2 us
    dot_general x4, matrix products, term(): lax.dot_general(out_weight, rows_input, (((0,), (1,)), ((), ())), preferr...  69.3 us
    all_to_all x3, waiting for transfers between devices, body(): lax.all_to_all(send_expand[:, step_index], 'pool', split_axis=0, concat_a...  51.3 us
    all_to_all x1, blocking collectives, body(): lax.all_to_all(send_expand[:, step_index], 'pool', split_axis=0, concat_a...  30.1 us
    psum x1, blocking collectives, body(): code_total = lax.psum(chosen, 'tp').astype(jnp.bfloat16)  22.3 us
    all_to_all x3, starting transfers between devices, body(): lax.all_to_all(send_expand[:, step_index], 'pool', split_axis=0, concat_a...  13.5 us
    gather x4, local copies, waits for them, and re-layouts, body(): recv_shrink.reshape(pool_size * CAP, rank_size, feature_shard)  12.9 us
    gather x4, local copies, waits for them, and re-layouts, body(): recv_expand.reshape(pool_size * CAP, rank_size, feature_shard)  11.5 us
  transfers between devices with their start and end apart: 8, of which 3 were waited for; matrix products, arithmetic and copies ran while one was open for 33% of the time, Pallas kernels for 0%

commit v1 on v0

v1 whole, which is shorter than its diff:
```python
import functools

import jax
import jax.numpy as jnp
from jax import lax
from jax.experimental import pallas as pl
from jax.experimental.pallas import tpu as pltpu
from jax.sharding import PartitionSpec as P

adapter_scale = 2.0
LANES = 128
HALVES = 2


def lane_parts(shape, rank):
    lane = lax.broadcasted_iota(jnp.int32, shape, 1)
    return lane // rank, lane < rank


def shrink_kernel(count, rank, *refs):
    rows_refs = refs[:count]
    place_ref, store_ref, out_ref = refs[count:]
    block = store_ref.shape[0]
    length = rows_refs[0].shape[0]
    step = pl.program_id(0)
    part, low = lane_parts((length, LANES), rank)
    per_group = LANES // rank
    first = step * (block // rank)
    for pair in range(count // 2):
        folded = []
        for side in range(2):
            index = 2 * pair + side
            place = place_ref[pl.ds(index * length, length), :] - first
            codes = lax.dot_general(
                rows_refs[index][...],
                store_ref[...],
                (((1,), (1,)), ((), ())),
                preferred_element_type=jnp.float32,
            )
            picked = jnp.zeros((length, LANES), jnp.float32)
            for group in range(block // LANES):
                picked += jnp.where(
                    part + group * per_group == place,
                    codes[:, group * LANES : (group + 1) * LANES],
                    0.0,
                )
            folded.append(picked + pltpu.roll(picked, rank, 1))
        packed = jnp.where(low, folded[0], folded[1])
        where_to = pl.ds(pair * length, length)

        @pl.when(step == 0)
        def _():
            out_ref[where_to, :] = packed

        @pl.when(step > 0)
        def _():
            out_ref[where_to, :] += packed


def shrink(rows, places, store, rank):
    count, (length, features) = len(rows), rows[0].shape
    width = store.shape[0]
    block = min(256, width)
    whole = lambda array: pl.BlockSpec(array.shape, lambda i: (0, 0))
    out = jax.ShapeDtypeStruct((count // 2 * length, LANES), jnp.float32)
    return pl.pallas_call(
        functools.partial(shrink_kernel, count, rank),
        grid=(width // block,),
        in_specs=[whole(r) for r in rows]
        + [whole(places), pl.BlockSpec((block, features), lambda i: (i, 0))],
        out_specs=whole(out),
        out_shape=out,
        compiler_params=pltpu.CompilerParams(
            dimension_semantics=("arbitrary",), vmem_limit_bytes=40 * 2**20
        ),
        cost_estimate=pl.CostEstimate(
            flops=2 * count * length * features * width,
            bytes_accessed=2 * features * (count * length + width),
            transcendentals=0,
        ),
        name="shrink",
    )(*rows, places, store)


def expand_kernel(count, rank, place_ref, code_ref, store_ref, *out_refs):
    width = store_ref.shape[0]
    length = out_refs[0].shape[0]
    part, low = lane_parts((length, LANES), rank)
    per_group = LANES // rank
    for pair in range(count // 2):
        code = code_ref[pl.ds(pair * length, length), :].astype(jnp.bfloat16).astype(jnp.float32)
        turned = pltpu.roll(code, rank, 1)
        for side in range(2):
            index = 2 * pair + side
            place = place_ref[pl.ds(index * length, length), :]
            both = jnp.where(low, code, turned) if side == 0 else jnp.where(low, turned, code)
            spread = jnp.concatenate(
                [
                    jnp.where(part + group * per_group == place, both, 0.0).astype(jnp.bfloat16)
                    for group in range(width // LANES)
                ],
                axis=1,
            )
            out_refs[index][...] = jnp.dot(
                spread, store_ref[...], preferred_element_type=jnp.float32
            ).astype(jnp.bfloat16)


def expand(codes, places, store, rank, count):
    width, features = store.shape
    length = codes.shape[0] // (count // 2)
    block = min(512, features)
    whole = lambda array: pl.BlockSpec(array.shape, lambda i: (0, 0))
    return pl.pallas_call(
        functools.partial(expand_kernel, count, rank),
        grid=(features // block,),
        in_specs=[whole(places), whole(codes), pl.BlockSpec((width, block), lambda i: (0, i))],
        out_specs=[pl.BlockSpec((length, block), lambda i: (0, i))] * count,
        out_shape=[jax.ShapeDtypeStruct((length, features), jnp.bfloat16)] * count,
        compiler_params=pltpu.CompilerParams(
            dimension_semantics=("arbitrary",), vmem_limit_bytes=40 * 2**20
        ),
        cost_estimate=pl.CostEstimate(
            flops=2 * count * length * features * width,
            bytes_accessed=2 * features * (count * length + width),
            transcendentals=0,
        ),
        name="expand",
    )(places, codes, store)


def body(inputs, out_weight, shrink_store, expand_store, owner_map, requests, row_slot):
    steps_count, rows_count, feature_shard = inputs.shape
    stored, rank = shrink_store.shape[:2]
    slot_count = requests.shape[2]
    pool_size, tp_size = lax.axis_size("pool"), lax.axis_size("tp")
    chips = pool_size // 2
    my_pool, my_tp = lax.axis_index("pool"), lax.axis_index("tp")
    my_chip, my_core = my_pool // 2, my_pool % 2
    all_rows = steps_count * rows_count
    flat = inputs.reshape(all_rows, feature_shard)
    shrink_flat = shrink_store.reshape(stored * rank, feature_shard)
    expand_flat = expand_store.reshape(stored * rank, feature_shard)

    swap = [(p, p ^ 1) for p in range(pool_size)]
    shift = lambda k: [(p, (p // 2 + k) % chips * 2 + p % 2) for p in range(pool_size)]
    around = [(i, (i + 1) % tp_size) for i in range(tp_size)]

    per_half = all_rows // HALVES
    halves = [flat[h * per_half : (h + 1) * per_half] for h in range(HALVES)]

    mine = [[half] + [lax.ppermute(half, "pool", shift(k)) for k in range(1, chips)] for half in halves]
    theirs = [[lax.ppermute(part, "pool", swap) for part in group] for group in mine]

    ids = jnp.arange(owner_map.shape[0], dtype=jnp.int32)
    positions = jnp.sum(
        jnp.where(requests[:, 0, :, None] == ids, owner_map, 0), axis=-1
    )
    slots = jnp.arange(slot_count, dtype=jnp.int32)
    row_position = jnp.sum(
        jnp.where(row_slot[:, :, None] == slots, positions[:, None, :], 0), axis=-1
    )
    every = lax.all_gather(row_position.reshape(1, all_rows), "pool", axis=0, tiled=True)
    every = every - my_pool * stored

    def places(h):
        found = []
        for core in (my_core, 1 - my_core):
            for k in range(chips):
                source = (my_chip - k + chips) % chips * 2 + core
                found.append(
                    lax.dynamic_slice(every, (source, h * per_half), (1, per_half))[0]
                )
        return jnp.broadcast_to(jnp.concatenate(found)[:, None], (pool_size * per_half, LANES))

    def base_part(back):
        target = (my_tp - back + tp_size) % tp_size
        columns = lax.dynamic_slice(
            out_weight, (0, target * feature_shard), (out_weight.shape[0], feature_shard)
        )
        return jnp.dot(flat, columns, preferred_element_type=jnp.float32)

    cut = lambda array, s: array[s * rows_count : (s + 1) * rows_count]
    part = base_part(1)
    moving = [cut(part, s).astype(jnp.bfloat16) for s in range(steps_count)]
    for back in range(2, tp_size + 1):
        part = base_part(back)
        moving = [
            cut(part, s) + lax.ppermute(moving[s], "tp", around).astype(jnp.float32)
            for s in range(steps_count)
        ]
        if back < tp_size:
            moving = [m.astype(jnp.bfloat16) for m in moving]

    updates = []
    for h in range(HALVES):
        place = places(h)
        codes = shrink(mine[h] + theirs[h], place, shrink_flat, rank)
        codes = lax.psum(codes, "tp")
        terms = expand(codes, place, expand_flat, rank, pool_size)
        total = None
        for k in range(chips):
            joined = terms[k] + lax.ppermute(terms[chips + k], "pool", swap)
            if k > 0:
                joined = lax.ppermute(joined, "pool", shift(chips - k))
            total = joined if total is None else total + joined
        updates.append(total)

    per = steps_count // HALVES
    rows_out = [
        (
            moving[s]
            + adapter_scale * cut(updates[s // per], s % per).astype(jnp.float32)
        ).astype(jnp.bfloat16)
        for s in range(steps_count)
    ]
    return jnp.stack(rows_out, axis=0)


def solution(mesh):
    placed = (
        P(None, ("groups", "pool"), "tp"),
        P("tp", None),
        P(("groups", "pool"), None, "tp"),
        P(("groups", "pool"), None, "tp"),
        P("groups"),
        P(None, ("groups", "pool"), None),
        P(None, ("groups", "pool")),
    )
    return jax.shard_map(
        body,
        mesh=mesh,
        in_specs=placed,
        out_specs=P(None, ("groups", "pool"), "tp"),
        check_vma=False,
    )
```

time: 382 us -> 257 us (0.67)
  blocking collectives: 145 us -> 5.34 us
  waiting for transfers between devices: 53.3 us -> 134 us
  matrix products: 88.8 us -> 32.8 us
  local copies, waits for them, and re-layouts: 52 us -> 10.2 us
  Pallas kernels: 0 us -> 29.6 us
  starting transfers between devices: 18.5 us -> 24.2 us
    all_to_all x4 -> x0, blocking collectives: 116 us -> none  [the longest x3 86.2 us: body(): lax.all_to_all(send_shrink[:, step_index], 'pool', split_axis=0, concat_a...]
    ppermute x0 -> x24, waiting for transfers between devices: none -> 103 us  [the longest x12 60.8 us: body(): lax.ppermute(moving[s], 'tp', around).astype(jnp.float32)]
    dot_general x12 -> x4, matrix products: 88.8 us -> 32.8 us  [base_part(): return jnp.dot(flat, columns, preferred_element_type=jnp.float32)]
    all_to_all x4 -> x0, waiting for transfers between devices: 53.2 us -> none  [the longest x3 51.3 us: body(): lax.all_to_all(send_expand[:, step_index], 'pool', split_axis=0, concat_a...]
    gather x10 -> x0, local copies, waits for them, and re-layouts: 38.8 us -> none  [the longest x4 12.9 us: body(): recv_shrink.reshape(pool_size * CAP, rank_size, feature_shard)]
    psum x0 -> x1, waiting for transfers between devices: none -> 31.5 us  [body(): codes = lax.psum(codes, 'tp')]
    pallas_call x0 -> x4, Pallas kernels: none -> 29.6 us  [the longest x2 18 us: shrink(): pl.pallas_call(functools.partial(shrink_kernel, count, rank), grid=(width...]
    ppermute x0 -> x24, starting transfers between devices: none -> 24.2 us  [the longest x12 17.1 us: body(): lax.ppermute(moving[s], 'tp', around).astype(jnp.float32)]
  transfers between devices with their start and end apart: 8 -> 25, of which waited for: 3 -> 12; matrix products, arithmetic and copies ran while one was open for 33% -> 15% of each run, Pallas kernels for 0% -> 12%
where the time goes in v1:
time: 257 us
  waiting for transfers between devices  134 us (52%)
  matrix products  32.8 us (13%)
  Pallas kernels  29.6 us (12%)
  starting transfers between devices  24.2 us (9%)
  between operations  13.7 us (5%)
  local copies, waits for them, and re-layouts  10.2 us (4%)
  other arithmetic  7.01 us (3%)
  blocking collectives  5.34 us (2%)
    ppermute x12, waiting for transfers between devices, body(): lax.ppermute(moving[s], 'tp', around).astype(jnp.float32)  60.8 us
    dot_general x4, matrix products, base_part(): return jnp.dot(flat, columns, preferred_element_type=jnp.float32)  32.8 us
    ppermute x2, waiting for transfers between devices, body(): lax.ppermute(half, 'pool', shift(k))  32.7 us
    psum x1, waiting for transfers between devices, body(): codes = lax.psum(codes, 'tp')  31.5 us
    pallas_call x2, Pallas kernels, shrink(): pl.pallas_call(functools.partial(shrink_kernel, count, rank), grid=(width...  18 us
    ppermute x12, starting transfers between devices, body(): lax.ppermute(moving[s], 'tp', around).astype(jnp.float32)  17.1 us
    pallas_call x2, Pallas kernels, expand(): pl.pallas_call(functools.partial(expand_kernel, count, rank), grid=(featu...  11.6 us
    ppermute x2, waiting for transfers between devices, body(): joined = lax.ppermute(joined, 'pool', shift(chips - k))  9.17 us
  transfers between devices with their start and end apart: 25, of which 12 were waited for; matrix products, arithmetic and copies ran while one was open for 15% of the time, Pallas kernels for 12%

profile of v1, /device:TPU:0, one launch (start us, length us, event | category | flops | bytes accessed | tf_op | source)
XLA Modules:
  0.0 257.1 jit_solution(5424851244064149895)
XLA Ops:
  6.5 1.7 fusion.48
  8.2 3.0 %collective-permute-start.3 = (bf16[256,2048]{1,0:T(8,128)(2,1)S(1)}, bf16[256,2048]{1,0:T(8,128)(2,1)S(1)}, u32[]{:S(2)}, u32[]{:S(2)}) collective-permute-start(bf16[256,2048]{1,0:T(8,128)(2,1)S(1)} %bitcast.38), channel_id=1, source_target_pairs={{0,8},{4,12},{8,0},{12,4},{1,9},{5,13},{9,1},{13,5},{2,10},{6,14},... | collective-permute-start | bytes 3145736 | tf_op jit(solution)/shard_map/ppermute | solution.py:152
  11.7 8.5 %fusion.20 = bf16[512,2048]{1,0:T(8,128)(2,1)S(1)} fusion(bf16[512,2048]{1,0:T(8,128)(2,1)} %bitcast.45, bf16[2048,8192]{1,0:T(8,128)(2,1)} %param.8, s32[]{:T(128)S(6)} %select_n.90), kind=kOutput, calls=%fused_computation.12 | convolution fusion | flops 4296015872 | bytes 12582916 | tf_op jit(solution)/shard_map/dot_general | solution.py:181
  20.3 14.9 %collective-permute-done.3.refs_1_ = bf16[256,2048]{1,0:T(8,128)(2,1)S(1)} collective-permute-done((bf16[256,2048]{1,0:T(8,128)(2,1)S(1)}, bf16[256,2048]{1,0:T(8,128)(2,1)S(1)}, u32[]{:S(2)}, u32[]{:S(2)}) %collective-permute-start.3) | collective-permute-done | bytes 1048608 | tf_op jit(solution)/shard_map/ppermute | solution.py:152
  35.2 1.6 fusion.47
  36.8 2.1 collective-permute-start
  39.2 17.8 %collective-permute-done.15.refs_1_ = bf16[256,2048]{1,0:T(8,128)(2,1)} collective-permute-done((bf16[256,2048]{1,0:T(8,128)(2,1)S(1)}, bf16[256,2048]{1,0:T(8,128)(2,1)}, u32[]{:S(2)}, u32[]{:S(2)}) %collective-permute-start.15) | collective-permute-done | bytes 1048608 | tf_op jit(solution)/shard_map/ppermute | solution.py:152
  57.0 5.3 %all-gather = s32[4,1,512]{2,1,0:T(1,128)S(1)} all-gather(s32[1,1,512]{2,1,0:T(1,128)S(1)} %bitcast.49), channel_id=1, replica_groups=mesh['groups'=2,'pool'=4,'tp'=4] {'pool'}, dimensions={0}, use_global_device_ids=true | all-gather | bytes 10240 | tf_op jit(solution)/shard_map/all_gather | solution.py:163
  62.4 1.7 collective-permute-start.12
  64.1 1.6 collective-permute-start.21
  65.9 2.2 copy-done
  69.3 9.1 %shrink.2 = f32[512,128]{1,0:T(8,128)} custom-call(bf16[256,2048]{1,0:T(8,128)(2,1)S(1)} %bitcast.40, bf16[256,2048]{1,0:T(8,128)(2,1)S(1)} %copy-done.5, bf16[256,2048]{1,0:T(8,128)(2,1)} %collective-permute-done.4.refs_2_, bf16[256,2048]{1,0:T(8,128)(2,1)} %collective-permute-done.5.refs_3_, s32[1024,128]{1,0:T(8,128)S(1)} %broadcast_in_dim.40.refs_4_.place_ref, ...), custom_call_target="tpu_custom_call" | custom-call | flops 4294967296 | bytes 8388608 | tf_op jit(solution)/shard_map/shrink/pallas_call | solution.py:66
  80.2 8.9 %shrink.3 = f32[512,128]{1,0:T(8,128)} custom-call(bf16[256,2048]{1,0:T(8,128)(2,1)S(1)} %bitcast.37, bf16[256,2048]{1,0:T(8,128)(2,1)} %collective-permute-done.15.refs_1_, bf16[256,2048]{1,0:T(8,128)(2,1)} %collective-permute-done.16.refs_2_, bf16[256,2048]{1,0:T(8,128)(2,1)S(1)} %collective-permute-done.17.refs_3_, ...), custom_call_target="tpu_custom_call" | custom-call | flops 4294967296 | bytes 8388608 | tf_op jit(solution)/shard_map/shrink/pallas_call | solution.py:66
  89.1 10.5 %fusion.14 = f32[512,2048]{1,0:T(8,128)} fusion(bf16[512,2048]{1,0:T(8,128)(2,1)} %bitcast.46, bf16[2048,8192]{1,0:T(8,128)(2,1)} %param.8, s32[]{:T(128)S(6)} %select_n.88), kind=kOutput, calls=%fused_computation.10 | convolution fusion | flops 4294967296 | bytes 14680068 | tf_op jit(solution)/shard_map/dot_general | solution.py:181
  99.6 31.5 %all-reduce.3.cloned.1.call-done = (f32[512,128]{1,0:T(8,128)}, f32[512,128]{1,0:T(8,128)}) async-done(((f32[512,128]{1,0:T(8,128)}, f32[512,128]{1,0:T(8,128)}), (f32[512,128]{1,0:T(8,128)}, f32[512,128]{1,0:T(8,128)})) %all-reduce.3.cloned.1.call-update) | async-done | bytes 524304 | tf_op jit(solution)/shard_map/psum | solution.py:199
  131.1 2.2 copy-done.2
  134.3 5.8 %expand.3 = (bf16[256,2048]{1,0:T(8,128)(2,1)S(1)}, bf16[256,2048]{1,0:T(8,128)(2,1)S(1)}, bf16[256,2048]{1,0:T(8,128)(2,1)S(1)}, bf16[256,2048]{1,0:T(8,128)(2,1)S(1)}) custom-call(s32[1024,128]{1,0:T(8,128)S(1)} %broadcast_in_dim.41.refs_4_.place_ref, f32[512,128]{1,0:T(8,128)S(1)} %copy-done.7, bf16[1024,2048]{1,0:T(8,128)(2,1)S(1)} %bitcast.43), custom_call_target="tpu_custom_call" | custom-call | flops 4294967296 | bytes 8388608 | tf_op jit(solution)/shard_map/expand/pallas_call | solution.py:114
  140.2 5.8 %expand.2 = (bf16[256,2048]{1,0:T(8,128)(2,1)S(1)}, bf16[256,2048]{1,0:T(8,128)(2,1)S(1)}, bf16[256,2048]{1,0:T(8,128)(2,1)S(1)}, bf16[256,2048]{1,0:T(8,128)(2,1)S(1)}) custom-call(s32[1024,128]{1,0:T(8,128)S(1)} %broadcast_in_dim.40.refs_4_.place_ref, f32[512,128]{1,0:T(8,128)S(1)} %copy-done.6, bf16[1024,2048]{1,0:T(8,128)(2,1)S(1)} %bitcast.44), custom_call_target="tpu_custom_call" | custom-call | flops 4294967296 | bytes 8388608 | tf_op jit(solution)/shard_map/expand/pallas_call | solution.py:114
  146.6 2.1 fusion.35
  150.1 6.9 %fusion.11 = f32[512,2048]{1,0:T(8,128)S(1)} fusion(bf16[512,2048]{1,0:T(8,128)(2,1)S(1)} %bitcast.47, bf16[2048,8192]{1,0:T(8,128)(2,1)} %param.8, s32[]{:T(128)S(6)} %select_n.86), kind=kOutput, calls=%fused_computation.9 | convolution fusion | flops 4294967296 | bytes 14680068 | tf_op jit(solution)/shard_map/dot_general | solution.py:181
  161.1 4.2 %collective-permute-done.1 = bf16[128,2048]{1,0:T(8,128)(2,1)S(1)} collective-permute-done((bf16[128,2048]{1,0:T(8,128)(2,1)S(1)}, bf16[128,2048]{1,0:T(8,128)(2,1)S(1)}, u32[]{:S(2)}, u32[]{:S(2)}) %collective-permute-start.1) | collective-permute-done | bytes 524320 | tf_op jit(solution)/shard_map/ppermute | solution.py:189
  166.8 6.9 %fusion.8 = f32[512,2048]{1,0:T(8,128)S(1)} fusion(bf16[512,2048]{1,0:T(8,128)(2,1)S(1)} %bitcast.48, bf16[2048,8192]{1,0:T(8,128)(2,1)} %param.8, s32[]{:T(128)S(6)} %select_n.84), kind=kOutput, calls=%fused_computation.8 | convolution fusion | flops 4294967296 | bytes 14680068 | tf_op jit(solution)/shard_map/dot_general | solution.py:181
  174.2 2.4 collective-permute-done.10
  176.6 11.2 %collective-permute-done.13 = bf16[128,2048]{1,0:T(8,128)(2,1)S(1)} collective-permute-done((bf16[128,2048]{1,0:T(8,128)(2,1)S(1)}, bf16[128,2048]{1,0:T(8,128)(2,1)S(1)}, u32[]{:S(2)}, u32[]{:S(2)}) %collective-permute-start.13) | collective-permute-done | bytes 524320 | tf_op jit(solution)/shard_map/ppermute | solution.py:189
  189.3 8.9 %collective-permute-done.22 = bf16[128,2048]{1,0:T(8,128)(2,1)S(1)} collective-permute-done((bf16[128,2048]{1,0:T(8,128)(2,1)S(1)}, bf16[128,2048]{1,0:T(8,128)(2,1)S(1)}, u32[]{:S(2)}, u32[]{:S(2)}) %collective-permute-start.22) | collective-permute-done | bytes 524320 | tf_op jit(solution)/shard_map/ppermute | solution.py:189
  200.9 3.3 %collective-permute-start.23 = (bf16[128,2048]{1,0:T(8,128)(2,1)S(1)}, bf16[128,2048]{1,0:T(8,128)(2,1)S(1)}, u32[]{:S(2)}, u32[]{:S(2)}) collective-permute-start(bf16[128,2048]{1,0:T(8,128)(2,1)S(1)} %get-tuple-element.30), channel_id=1, source_target_pairs={{0,1},{1,2},{2,3},{3,0},{4,5},{5,6},{6,7},{7,4},{8,9},{9,10},{10,1... | collective-permute-start | bytes 1572872 | tf_op jit(solution)/shard_map/ppermute | solution.py:189
  204.2 9.2 %collective-permute-done.8 = bf16[256,2048]{1,0:T(8,128)(2,1)S(1)} collective-permute-done((bf16[256,2048]{1,0:T(8,128)(2,1)S(1)}, bf16[256,2048]{1,0:T(8,128)(2,1)S(1)}, u32[]{:S(2)}, u32[]{:S(2)}) %collective-permute-start.8) | collective-permute-done | bytes 1048608 | tf_op jit(solution)/shard_map/ppermute | solution.py:205
  213.6 2.1 collective-permute-done.11
  215.7 11.2 %collective-permute-done.14 = bf16[128,2048]{1,0:T(8,128)(2,1)S(1)} collective-permute-done((bf16[128,2048]{1,0:T(8,128)(2,1)S(1)}, bf16[128,2048]{1,0:T(8,128)(2,1)S(1)}, u32[]{:S(2)}, u32[]{:S(2)}) %collective-permute-start.14) | collective-permute-done | bytes 524320 | tf_op jit(solution)/shard_map/ppermute | solution.py:189
  226.9 11.2 %collective-permute-done.2 = bf16[128,2048]{1,0:T(8,128)(2,1)S(1)} collective-permute-done((bf16[128,2048]{1,0:T(8,128)(2,1)S(1)}, bf16[128,2048]{1,0:T(8,128)(2,1)S(1)}, u32[]{:S(2)}, u32[]{:S(2)}) %collective-permute-start.2) | collective-permute-done | bytes 524320 | tf_op jit(solution)/shard_map/ppermute | solution.py:189
  238.1 9.5 %collective-permute-done.23 = bf16[128,2048]{1,0:T(8,128)(2,1)S(1)} collective-permute-done((bf16[128,2048]{1,0:T(8,128)(2,1)S(1)}, bf16[128,2048]{1,0:T(8,128)(2,1)S(1)}, u32[]{:S(2)}, u32[]{:S(2)}) %collective-permute-start.23) | collective-permute-done | bytes 524320 | tf_op jit(solution)/shard_map/ppermute | solution.py:189
  248.7 1.6 pad_maximum_fusion
  (72 shorter events, 18.4 us)
Async XLA Ops:
  6.5 124.6 %all-reduce.3.cloned.1.call-start = ((), (), s32[]{:S(2)}) async-start(), calls=%async_computation | async-start | bytes 1048576 | tf_op jit(solution)/shard_map/psum | solution.py:199
  8.2 27.0 %collective-permute-start.3 = (bf16[256,2048]{1,0:T(8,128)(2,1)S(1)}, bf16[256,2048]{1,0:T(8,128)(2,1)S(1)}, u32[]{:S(2)}, u32[]{:S(2)}) collective-permute-start(bf16[256,2048]{1,0:T(8,128)(2,1)S(1)} %bitcast.38), channel_id=1, source_target_pairs={{0,8},{4,12},{8,0},{12,4},{1,9},{5,13},{9,1},{13,5},{2,10},{6,14},... | collective-permute-start | bytes 3145736 | tf_op jit(solution)/shard_map/ppermute | solution.py:152
  11.2 51.2 %collective-permute-start.4 = (bf16[256,2048]{1,0:T(8,128)(2,1)S(1)}, bf16[256,2048]{1,0:T(8,128)(2,1)}, u32[]{:S(2)}, u32[]{:S(2)}) collective-permute-start(bf16[256,2048]{1,0:T(8,128)(2,1)S(1)} %bitcast.39), channel_id=1, source_target_pairs={{0,4},{4,0},{8,12},{12,8},{1,5},{5,1},{9,13},{13,9},{2,6},{6,2},{1... | collective-permute-start | bytes 3145736 | tf_op jit(solution)/shard_map/ppermute | solution.py:153
  11.2 45.7 %collective-permute-start.15 = (bf16[256,2048]{1,0:T(8,128)(2,1)S(1)}, bf16[256,2048]{1,0:T(8,128)(2,1)}, u32[]{:S(2)}, u32[]{:S(2)}) collective-permute-start(bf16[256,2048]{1,0:T(8,128)(2,1)S(1)} %bitcast.35), channel_id=1, source_target_pairs={{0,8},{4,12},{8,0},{12,4},{1,9},{5,13},{9,1},{13,5},{2,10},{6,14},... | collective-permute-start | bytes 3145736 | tf_op jit(solution)/shard_map/ppermute | solution.py:152
  11.4 67.0 %collective-permute-start.16 = (bf16[256,2048]{1,0:T(8,128)(2,1)S(1)}, bf16[256,2048]{1,0:T(8,128)(2,1)}, u32[]{:S(2)}, u32[]{:S(2)}) collective-permute-start(bf16[256,2048]{1,0:T(8,128)(2,1)S(1)} %bitcast.36), channel_id=1, source_target_pairs={{0,4},{4,0},{8,12},{12,8},{1,5},{5,1},{9,13},{13,9},{2,6},{6,2},{1... | collective-permute-start | bytes 3145736 | tf_op jit(solution)/shard_map/ppermute | solution.py:153
  20.2 18.7 %copy-start.11 = (s32[4,1,8]{2,1,0:T(1,128)S(1)}, s32[4,1,8]{2,1,0:T(1,128)}, u32[]{:S(2)}) copy-start(s32[4,1,8]{2,1,0:T(1,128)} %param.12) | copy-start | bytes 388
  20.3 18.7 %copy-start.12 = (s32[64]{0:T(128)S(1)}, s32[64]{0:T(128)}, u32[]{:S(2)}) copy-start(s32[64]{0:T(128)} %param.11) | copy-start | bytes 772
  20.3 36.7 %copy-start.10 = (s32[4,128]{1,0:T(4,128)S(1)}, s32[4,128]{1,0:T(4,128)}, u32[]{:S(2)}) copy-start(s32[4,128]{1,0:T(4,128)} %param.13) | copy-start | bytes 6148
  35.2 28.9 %copy-start.4 = (bf16[256,2048]{1,0:T(8,128)(2,1)}, bf16[256,2048]{1,0:T(8,128)(2,1)S(1)}, u32[]{:S(2)}) copy-start(bf16[256,2048]{1,0:T(8,128)(2,1)S(1)} %collective-permute-done.3.refs_1_) | copy-start | bytes 3145732
  35.2 28.9 %collective-permute-start.5 = (bf16[256,2048]{1,0:T(8,128)(2,1)S(1)}, bf16[256,2048]{1,0:T(8,128)(2,1)}, u32[]{:S(2)}, u32[]{:S(2)}) collective-permute-start(bf16[256,2048]{1,0:T(8,128)(2,1)S(1)} %collective-permute-done.3.refs_1_), channel_id=1, source_target_pairs={{0,4},{4,0},{8,12},{12,8},{1,5},{5,1},{9,13},{13,9},{2,6},{6,2},{1... | collective-permute-start | bytes 3145736 | tf_op jit(solution)/shard_map/ppermute | solution.py:153
  36.8 109.2 %collective-permute-start = (bf16[128,2048]{1,0:T(8,128)(2,1)}, bf16[128,2048]{1,0:T(8,128)(2,1)}, u32[]{:S(2)}, u32[]{:S(2)}) collective-permute-start(bf16[128,2048]{1,0:T(8,128)(2,1)} %get-tuple-element.37), channel_id=1, source_target_pairs={{0,1},{1,2},{2,3},{3,0},{4,5},{5,6},{6,7},{7,4},{8,9},{9,10},{10,1... | collective-permute-start | bytes 1572872 | tf_op jit(solution)/shard_map/ppermute | solution.py:189
  57.0 23.0 %collective-permute-start.17 = (bf16[256,2048]{1,0:T(8,128)(2,1)}, bf16[256,2048]{1,0:T(8,128)(2,1)S(1)}, u32[]{:S(2)}, u32[]{:S(2)}) collective-permute-start(bf16[256,2048]{1,0:T(8,128)(2,1)} %collective-permute-done.15.refs_1_), channel_id=1, source_target_pairs={{0,4},{4,0},{8,12},{12,8},{1,5},{5,1},{9,13},{13,9},{2,6},{6,2},{1... | collective-permute-start | bytes 3145736 | tf_op jit(solution)/shard_map/ppermute | solution.py:153
  62.4 84.1 %collective-permute-start.12 = (bf16[128,2048]{1,0:T(8,128)(2,1)}, bf16[128,2048]{1,0:T(8,128)(2,1)}, u32[]{:S(2)}, u32[]{:S(2)}) collective-permute-start(bf16[128,2048]{1,0:T(8,128)(2,1)} %get-tuple-element.39), channel_id=1, source_target_pairs={{0,1},{1,2},{2,3},{3,0},{4,5},{5,6},{6,7},{7,4},{8,9},{9,10},{10,1... | collective-permute-start | bytes 1572872 | tf_op jit(solution)/shard_map/ppermute | solution.py:189
  64.1 82.4 %collective-permute-start.21 = (bf16[128,2048]{1,0:T(8,128)(2,1)}, bf16[128,2048]{1,0:T(8,128)(2,1)}, u32[]{:S(2)}, u32[]{:S(2)}) collective-permute-start(bf16[128,2048]{1,0:T(8,128)(2,1)} %get-tuple-element.38), channel_id=1, source_target_pairs={{0,1},{1,2},{2,3},{3,0},{4,5},{5,6},{6,7},{7,4},{8,9},{9,10},{10,1... | collective-permute-start | bytes 1572872 | tf_op jit(solution)/shard_map/ppermute | solution.py:189
  69.3 10.9 %copy-start.1 = (bf16[16,64,2048]{2,1,0:T(8,128)(2,1)S(1)}, bf16[16,64,2048]{2,1,0:T(8,128)(2,1)}, u32[]{:S(2)}) copy-start(bf16[16,64,2048]{2,1,0:T(8,128)(2,1)} %param.9) | copy-start | bytes 12582916
  78.4 68.1 %collective-permute-start.9 = (bf16[128,2048]{1,0:T(8,128)(2,1)}, bf16[128,2048]{1,0:T(8,128)(2,1)S(1)}, u32[]{:S(2)}, u32[]{:S(2)}) collective-permute-start(bf16[128,2048]{1,0:T(8,128)(2,1)} %get-tuple-element.40), channel_id=1, source_target_pairs={{0,1},{1,2},{2,3},{3,0},{4,5},{5,6},{6,7},{7,4},{8,9},{9,10},{10,1... | collective-permute-start | bytes 1572872 | tf_op jit(solution)/shard_map/ppermute | solution.py:189
  134.3 5.9 %copy-start.6 = (f32[512,128]{1,0:T(8,128)S(1)}, f32[512,128]{1,0:T(8,128)}, u32[]{:S(2)}) copy-start(f32[512,128]{1,0:T(8,128)} %get-tuple-element.22.code_ref) | copy-start | bytes 786436
  140.1 19.1 %collective-permute-start.19 = (bf16[256,2048]{1,0:T(8,128)(2,1)S(1)}, bf16[256,2048]{1,0:T(8,128)(2,1)S(1)}, u32[]{:S(2)}, u32[]{:S(2)}) collective-permute-start(bf16[256,2048]{1,0:T(8,128)(2,1)S(1)} %get-tuple-element.20), channel_id=1, source_target_pairs={{0,4},{4,0},{8,12},{12,8},{1,5},{5,1},{9,13},{13,9},{2,6},{6,2},{1... | collective-permute-start | bytes 3145736 | tf_op jit(solution)/shard_map/ppermute | solution.py:203
  140.2 6.4 %copy-start.8 = (f32[512,2048]{1,0:T(8,128)S(1)}, f32[512,2048]{1,0:T(8,128)}, u32[]{:S(2)}) copy-start(f32[512,2048]{1,0:T(8,128)} %fusion.14) | copy-start | bytes 12582916
  146.0 19.3 %collective-permute-start.7 = (bf16[256,2048]{1,0:T(8,128)(2,1)S(1)}, bf16[256,2048]{1,0:T(8,128)(2,1)S(1)}, u32[]{:S(2)}, u32[]{:S(2)}) collective-permute-start(bf16[256,2048]{1,0:T(8,128)(2,1)S(1)} %get-tuple-element.16), channel_id=1, source_target_pairs={{0,4},{4,0},{8,12},{12,8},{1,5},{5,1},{9,13},{13,9},{2,6},{6,2},{1... | collective-permute-start | bytes 3145736 | tf_op jit(solution)/shard_map/ppermute | solution.py:203
  148.7 16.6 %collective-permute-start.1 = (bf16[128,2048]{1,0:T(8,128)(2,1)S(1)}, bf16[128,2048]{1,0:T(8,128)(2,1)S(1)}, u32[]{:S(2)}, u32[]{:S(2)}) collective-permute-start(bf16[128,2048]{1,0:T(8,128)(2,1)S(1)} %get-tuple-element.33), channel_id=1, source_target_pairs={{0,1},{1,2},{2,3},{3,0},{4,5},{5,6},{6,7},{7,4},{8,9},{9,10},{10,1... | collective-permute-start | bytes 1572872 | tf_op jit(solution)/shard_map/ppermute | solution.py:189
  157.0 19.5 %collective-permute-start.10 = (bf16[128,2048]{1,0:T(8,128)(2,1)S(1)}, bf16[128,2048]{1,0:T(8,128)(2,1)S(1)}, u32[]{:S(2)}, u32[]{:S(2)}) collective-permute-start(bf16[128,2048]{1,0:T(8,128)(2,1)S(1)} %get-tuple-element.36), channel_id=1, source_target_pairs={{0,1},{1,2},{2,3},{3,0},{4,5},{5,6},{6,7},{7,4},{8,9},{9,10},{10,1... | collective-permute-start | bytes 1572872 | tf_op jit(solution)/shard_map/ppermute | solution.py:189
  158.4 29.4 %collective-permute-start.13 = (bf16[128,2048]{1,0:T(8,128)(2,1)S(1)}, bf16[128,2048]{1,0:T(8,128)(2,1)S(1)}, u32[]{:S(2)}, u32[]{:S(2)}) collective-permute-start(bf16[128,2048]{1,0:T(8,128)(2,1)S(1)} %get-tuple-element.35), channel_id=1, source_target_pairs={{0,1},{1,2},{2,3},{3,0},{4,5},{5,6},{6,7},{7,4},{8,9},{9,10},{10,1... | collective-permute-start | bytes 1572872 | tf_op jit(solution)/shard_map/ppermute | solution.py:189
  159.2 39.0 %collective-permute-start.22 = (bf16[128,2048]{1,0:T(8,128)(2,1)S(1)}, bf16[128,2048]{1,0:T(8,128)(2,1)S(1)}, u32[]{:S(2)}, u32[]{:S(2)}) collective-permute-start(bf16[128,2048]{1,0:T(8,128)(2,1)S(1)} %get-tuple-element.34), channel_id=1, source_target_pairs={{0,1},{1,2},{2,3},{3,0},{4,5},{5,6},{6,7},{7,4},{8,9},{9,10},{10,1... | collective-permute-start | bytes 1572872 | tf_op jit(solution)/shard_map/ppermute | solution.py:189
  165.3 33.7 %collective-permute-start.18 = (bf16[256,2048]{1,0:T(8,128)(2,1)S(1)}, bf16[256,2048]{1,0:T(8,128)(2,1)S(1)}, u32[]{:S(2)}, u32[]{:S(2)}) collective-permute-start(bf16[256,2048]{1,0:T(8,128)(2,1)S(1)} %get-tuple-element.18), channel_id=1, source_target_pairs={{0,4},{4,0},{8,12},{12,8},{1,5},{5,1},{9,13},{13,9},{2,6},{6,2},{1... | collective-permute-start | bytes 3145736 | tf_op jit(solution)/shard_map/ppermute | solution.py:203
  165.3 34.5 %collective-permute-start.20 = (bf16[256,2048]{1,0:T(8,128)(2,1)S(1)}, bf16[256,2048]{1,0:T(8,128)(2,1)S(1)}, u32[]{:S(2)}, u32[]{:S(2)}) collective-permute-start(bf16[256,2048]{1,0:T(8,128)(2,1)S(1)} %add.219), channel_id=1, source_target_pairs={{0,8},{4,12},{8,0},{12,4},{1,9},{5,13},{9,1},{13,5},{2,10},{6,14},... | collective-permute-start | bytes 3145736 | tf_op jit(solution)/shard_map/ppermute | solution.py:205
  176.6 24.3 %collective-permute-start.6 = (bf16[256,2048]{1,0:T(8,128)(2,1)S(1)}, bf16[256,2048]{1,0:T(8,128)(2,1)S(1)}, u32[]{:S(2)}, u32[]{:S(2)}) collective-permute-start(bf16[256,2048]{1,0:T(8,128)(2,1)S(1)} %get-tuple-element.14), channel_id=1, source_target_pairs={{0,4},{4,0},{8,12},{12,8},{1,5},{5,1},{9,13},{13,9},{2,6},{6,2},{1... | collective-permute-start | bytes 3145736 | tf_op jit(solution)/shard_map/ppermute | solution.py:203
  187.8 25.6 %collective-permute-start.8 = (bf16[256,2048]{1,0:T(8,128)(2,1)S(1)}, bf16[256,2048]{1,0:T(8,128)(2,1)S(1)}, u32[]{:S(2)}, u32[]{:S(2)}) collective-permute-start(bf16[256,2048]{1,0:T(8,128)(2,1)S(1)} %add.208), channel_id=1, source_target_pairs={{0,8},{4,12},{8,0},{12,4},{1,9},{5,13},{9,1},{13,5},{2,10},{6,14},... | collective-permute-start | bytes 3145736 | tf_op jit(solution)/shard_map/ppermute | solution.py:205
  198.9 16.7 %collective-permute-start.11 = (bf16[128,2048]{1,0:T(8,128)(2,1)S(1)}, bf16[128,2048]{1,0:T(8,128)(2,1)S(1)}, u32[]{:S(2)}, u32[]{:S(2)}) collective-permute-start(bf16[128,2048]{1,0:T(8,128)(2,1)S(1)} %get-tuple-element.32), channel_id=1, source_target_pairs={{0,1},{1,2},{2,3},{3,0},{4,5},{5,6},{6,7},{7,4},{8,9},{9,10},{10,1... | collective-permute-start | bytes 1572872 | tf_op jit(solution)/shard_map/ppermute | solution.py:189
  199.0 27.9 %collective-permute-start.14 = (bf16[128,2048]{1,0:T(8,128)(2,1)S(1)}, bf16[128,2048]{1,0:T(8,128)(2,1)S(1)}, u32[]{:S(2)}, u32[]{:S(2)}) collective-permute-start(bf16[128,2048]{1,0:T(8,128)(2,1)S(1)} %get-tuple-element.31), channel_id=1, source_target_pairs={{0,1},{1,2},{2,3},{3,0},{4,5},{5,6},{6,7},{7,4},{8,9},{9,10},{10,1... | collective-permute-start | bytes 1572872 | tf_op jit(solution)/shard_map/ppermute | solution.py:189
  199.8 38.3 %collective-permute-start.2 = (bf16[128,2048]{1,0:T(8,128)(2,1)S(1)}, bf16[128,2048]{1,0:T(8,128)(2,1)S(1)}, u32[]{:S(2)}, u32[]{:S(2)}) collective-permute-start(bf16[128,2048]{1,0:T(8,128)(2,1)S(1)} %get-tuple-element.29), channel_id=1, source_target_pairs={{0,1},{1,2},{2,3},{3,0},{4,5},{5,6},{6,7},{7,4},{8,9},{9,10},{10,1... | collective-permute-start | bytes 1572872 | tf_op jit(solution)/shard_map/ppermute | solution.py:189
  200.9 46.7 %collective-permute-start.23 = (bf16[128,2048]{1,0:T(8,128)(2,1)S(1)}, bf16[128,2048]{1,0:T(8,128)(2,1)S(1)}, u32[]{:S(2)}, u32[]{:S(2)}) collective-permute-start(bf16[128,2048]{1,0:T(8,128)(2,1)S(1)} %get-tuple-element.30), channel_id=1, source_target_pairs={{0,1},{1,2},{2,3},{3,0},{4,5},{5,6},{6,7},{7,4},{8,9},{9,10},{10,1... | collective-permute-start | bytes 1572872 | tf_op jit(solution)/shard_map/ppermute | solution.py:189
  (6 other events, 16.5 us)
Sparse Core Ops, SparseCore 0:
  89.3 41.8 all-reduce.2

commit v2 on v1

--- a/solution.py
+++ b/solution.py
@@ -19,7 +19,7 @@
 
 def shrink_kernel(count, rank, *refs):
     rows_refs = refs[:count]
-    place_ref, store_ref, out_ref = refs[count:]
+    place_ref, store_ref, _, out_ref = refs[count:]
     block = store_ref.shape[0]
     length = rows_refs[0].shape[0]
     step = pl.program_id(0)
@@ -57,8 +57,12 @@
             out_ref[where_to, :] += packed
 
 
-def shrink(rows, places, store, rank):
-    count, (length, features) = len(rows), rows[0].shape
+def rows_block(length, features, index):
+    return pl.BlockSpec((length, features), lambda i: (index, 0))
+
+
+def shrink(rows, length, places, store, rank, token):
+    count, features = len(rows), store.shape[1]
     width = store.shape[0]
     block = min(256, width)
     whole = lambda array: pl.BlockSpec(array.shape, lambda i: (0, 0))
@@ -66,23 +70,27 @@
     return pl.pallas_call(
         functools.partial(shrink_kernel, count, rank),
         grid=(width // block,),
-        in_specs=[whole(r) for r in rows]
-        + [whole(places), pl.BlockSpec((block, features), lambda i: (i, 0))],
+        in_specs=[rows_block(length, features, index) for _, index in rows]
+        + [
+            whole(places),
+            pl.BlockSpec((block, features), lambda i: (i, 0)),
+            pl.BlockSpec(memory_space=pl.ANY),
+        ],
         out_specs=whole(out),
         out_shape=out,
         compiler_params=pltpu.CompilerParams(
             dimension_semantics=("arbitrary",), vmem_limit_bytes=40 * 2**20
         ),
         cost_estimate=pl.CostEstimate(
-            flops=2 * count * length * features * width,
-            bytes_accessed=2 * features * (count * length + width),
+            flops=count * length,
+            bytes_accessed=count * length,
             transcendentals=0,
         ),
         name="shrink",
-    )(*rows, places, store)
-
-
-def expand_kernel(count, rank, place_ref, code_ref, store_ref, *out_refs):
+    )(*[array for array, _ in rows], places, store, token)
+
+
+def expand_kernel(count, rank, place_ref, code_ref, store_ref, _, *out_refs):
     width = store_ref.shape[0]
     length = out_refs[0].shape[0]
     part, low = lane_parts((length, LANES), rank)
@@ -106,7 +114,7 @@
             ).astype(jnp.bfloat16)
 
 
-def expand(codes, places, store, rank, count):
+def expand(codes, places, store, rank, count, token):
     width, features = store.shape
     length = codes.shape[0] // (count // 2)
     block = min(512, features)
@@ -114,19 +122,52 @@
     return pl.pallas_call(
         functools.partial(expand_kernel, count, rank),
         grid=(features // block,),
-        in_specs=[whole(places), whole(codes), pl.BlockSpec((width, block), lambda i: (0, i))],
+        in_specs=[
+            whole(places),
+            whole(codes),
+            pl.BlockSpec((width, block), lambda i: (0, i)),
+            pl.BlockSpec(memory_space=pl.ANY),
+        ],
         out_specs=[pl.BlockSpec((length, block), lambda i: (0, i))] * count,
         out_shape=[jax.ShapeDtypeStruct((length, features), jnp.bfloat16)] * count,
         compiler_params=pltpu.CompilerParams(
             dimension_semantics=("arbitrary",), vmem_limit_bytes=40 * 2**20
         ),
         cost_estimate=pl.CostEstimate(
-            flops=2 * count * length * features * width,
-            bytes_accessed=2 * features * (count * length + width),
+            flops=count * length,
+            bytes_accessed=count * length,
             transcendentals=0,
         ),
         name="expand",
-    )(places, codes, store)
+    )(places, codes, store, token)
+
+
+def add_kernel(part_ref, moving_ref, _, out_ref):
+    out_ref[...] = (part_ref[...] + moving_ref[...].astype(jnp.float32)).astype(jnp.bfloat16)
+
+
+def add(part, moving, chunk, token):
+    length, features = moving.shape
+    pieces = 4
+    block = (length // pieces, features)
+    return pl.pallas_call(
+        add_kernel,
+        grid=(pieces,),
+        in_specs=[
+            pl.BlockSpec(block, lambda i: (chunk * pieces + i, 0)),
+            pl.BlockSpec(block, lambda i: (i, 0)),
+            pl.BlockSpec(memory_space=pl.ANY),
+        ],
+        out_specs=pl.BlockSpec(block, lambda i: (i, 0)),
+        out_shape=jax.ShapeDtypeStruct((length, features), jnp.bfloat16),
+        compiler_params=pltpu.CompilerParams(
+            dimension_semantics=("arbitrary",), vmem_limit_bytes=16 * 2**20
+        ),
+        cost_estimate=pl.CostEstimate(
+            flops=length, bytes_accessed=length, transcendentals=0
+        ),
+        name="add",
+    )(part, moving, token)
 
 
 def body(inputs, out_weight, shrink_store, expand_store, owner_map, requests, row_slot):
@@ -149,8 +190,13 @@
     per_half = all_rows // HALVES
     halves = [flat[h * per_half : (h + 1) * per_half] for h in range(HALVES)]
 
-    mine = [[half] + [lax.ppermute(half, "pool", shift(k)) for k in range(1, chips)] for half in halves]
-    theirs = [[lax.ppermute(part, "pool", swap) for part in group] for group in mine]
+    far = [[lax.ppermute(half, "pool", shift(k)) for k in range(1, chips)] for half in halves]
+    near = lax.ppermute(flat, "pool", swap)
+    far_near = [[lax.ppermute(part, "pool", swap) for part in group] for group in far]
+
+    def rows_of(h):
+        first = [(flat, h)] + [(part, 0) for part in far[h]]
+        return first + [(near, h)] + [(part, 0) for part in far_near[h]]
 
     ids = jnp.arange(owner_map.shape[0], dtype=jnp.int32)
     positions = jnp.sum(
@@ -180,41 +226,52 @@
         )
         return jnp.dot(flat, columns, preferred_element_type=jnp.float32)
 
-    cut = lambda array, s: array[s * rows_count : (s + 1) * rows_count]
-    part = base_part(1)
-    moving = [cut(part, s).astype(jnp.bfloat16) for s in range(steps_count)]
-    for back in range(2, tp_size + 1):
-        part = base_part(back)
-        moving = [
-            cut(part, s) + lax.ppermute(moving[s], "tp", around).astype(jnp.float32)
-            for s in range(steps_count)
-        ]
-        if back < tp_size:
-            moving = [m.astype(jnp.bfloat16) for m in moving]
-
-    updates = []
-    for h in range(HALVES):
-        place = places(h)
-        codes = shrink(mine[h] + theirs[h], place, shrink_flat, rank)
-        codes = lax.psum(codes, "tp")
-        terms = expand(codes, place, expand_flat, rank, pool_size)
-        total = None
+    cut = lambda array, h: array[h * per_half : (h + 1) * per_half]
+    parts = [base_part(back) for back in range(1, tp_size + 1)]
+    moving = [cut(parts[0], h).astype(jnp.bfloat16) for h in range(HALVES)]
+
+    def ring(back, h, token):
+        arrived = lax.ppermute(moving[h], "tp", around)
+        moving[h] = add(parts[back - 1], arrived, h, token)
+        return moving[h]
+
+    def update_of(terms):
+        total = last = None
         for k in range(chips):
             joined = terms[k] + lax.ppermute(terms[chips + k], "pool", swap)
             if k > 0:
+                last = joined
                 joined = lax.ppermute(joined, "pool", shift(chips - k))
             total = joined if total is None else total + joined
-        updates.append(total)
-
-    per = steps_count // HALVES
-    rows_out = [
-        (
-            moving[s]
-            + adapter_scale * cut(updates[s // per], s % per).astype(jnp.float32)
-        ).astype(jnp.bfloat16)
-        for s in range(steps_count)
-    ]
-    return jnp.stack(rows_out, axis=0)
+        return total, last
+
+    place = [places(h) for h in range(HALVES)]
+    token = moving[0]
+    codes = [None] * HALVES
+    steps = [(back, h) for back in range(2, tp_size) for h in range(HALVES)]
+    for h in range(HALVES):
+        codes[h] = token = shrink(rows_of(h), per_half, place[h], shrink_flat, rank, token)
+        if h > 0:
+            codes[h], _ = lax.optimization_barrier((codes[h], codes[h - 1]))
+        codes[h] = lax.psum(codes[h], "tp")
+        token = ring(*steps.pop(0), token)
+    updates = []
+    for h in range(HALVES):
+        terms = expand(codes[h], place[h], expand_flat, rank, pool_size, token)
+        update, token = update_of(terms)
+        updates.append(update)
+        if h == 0:
+            for _ in range(HALVES):
+                token = ring(*steps.pop(0), token)
+    for back, h in steps:
+        token = ring(back, h, token)
+
+    rows_out = []
+    for h in range(HALVES):
+        base = cut(parts[-1], h) + lax.ppermute(moving[h], "tp", around).astype(jnp.float32)
+        update = updates[h].astype(jnp.float32)
+        rows_out.append((base + adapter_scale * update).astype(jnp.bfloat16))
+    return jnp.concatenate(rows_out, axis=0).reshape(inputs.shape)
 
 
 def solution(mesh):

time: 257 us -> 286 us (1.11)
  blocking collectives: 5.34 us -> 33.5 us
  waiting for transfers between devices: 134 us -> 113 us
  Pallas kernels: 29.6 us -> 44.7 us
  local copies, waits for them, and re-layouts: 10.2 us -> 23.4 us
  starting transfers between devices: 24.2 us -> 15.2 us
  other arithmetic: 7.01 us -> 10.3 us
    ppermute x2, waiting for transfers between devices: 32.7 us -> 0.01 us  [body(): lax.ppermute(half, 'pool', shift(k))]
    all_gather x1, blocking collectives: 5.34 us -> 33.5 us  [body(): lax.all_gather(row_position.reshape(1, all_rows), 'pool', axis=0, tiled=T...]
    pallas_call x0 -> x4, Pallas kernels: none -> 13.7 us  [add(): pl.pallas_call(add_kernel, grid=(pieces,), in_specs=[pl.BlockSpec(block,...]
    unnamed x26 -> x44, local copies, waits for them, and re-layouts: 6.59 us -> 18 us
    ppermute x18 -> x13, starting transfers between devices: 20.7 us -> 12.1 us  [the longest x4 6.38 us: ring(): arrived = lax.ppermute(moving[h], 'tp', around)]
    ppermute x18 -> x13, waiting for transfers between devices: 70 us -> 75.5 us  [the longest x4 38.6 us: ring(): arrived = lax.ppermute(moving[h], 'tp', around)]
    psum x1 -> x2, waiting for transfers between devices: 31.5 us -> 36.9 us  [body(): codes[h] = lax.psum(codes[h], 'tp')]
  transfers between devices with their start and end apart: 25 -> 19, of which waited for: 12 -> 7; matrix products, arithmetic and copies ran while one was open for 15% -> 14% of each run, Pallas kernels for 12% -> 11%
where the time goes in v2:
time: 286 us
  waiting for transfers between devices  113 us (40%)
  Pallas kernels  44.7 us (16%)
  blocking collectives  33.5 us (12%)
  matrix products  31.6 us (11%)
  local copies, waits for them, and re-layouts  23.4 us (8%)
  starting transfers between devices  15.2 us (5%)
  between operations  13.6 us (5%)
  other arithmetic  10.3 us (4%)
    ppermute x4, waiting for transfers between devices, ring(): arrived = lax.ppermute(moving[h], 'tp', around)  38.6 us
    psum x2, waiting for transfers between devices, body(): codes[h] = lax.psum(codes[h], 'tp')  36.9 us
    ppermute x2, waiting for transfers between devices, body(): lax.ppermute(moving[h], 'tp', around).astype(jnp.float32)  36.5 us
    all_gather x1, blocking collectives, body(): lax.all_gather(row_position.reshape(1, all_rows), 'pool', axis=0, tiled=T...  33.5 us
    dot_general x4, matrix products, base_part(): return jnp.dot(flat, columns, preferred_element_type=jnp.float32)  31.6 us
    pallas_call x2, Pallas kernels, shrink(): pl.pallas_call(functools.partial(shrink_kernel, count, rank), grid=(width...  18.1 us
    unnamed x44, local copies, waits for them, and re-layouts  18 us
    pallas_call x4, Pallas kernels, add(): pl.pallas_call(add_kernel, grid=(pieces,), in_specs=[pl.BlockSpec(block,...  13.7 us
  transfers between devices with their start and end apart: 19, of which 7 were waited for; matrix products, arithmetic and copies ran while one was open for 14% of the time, Pallas kernels for 11%

profile of v2, /device:TPU:0, one launch (start us, length us, event | category | flops | bytes accessed | tf_op | source)
XLA Modules:
  0.0 285.5 jit_solution(10200719153789894002)
XLA Ops:
  7.0 3.3 %fusion.31 = (bf16[2,128,2048]{2,1,0:T(8,128)(2,1)}, bf16[2,128,2048]{2,1,0:T(8,128)(2,1)}) fusion(bf16[4,128,2048]{2,1,0:T(8,128)(2,1)} %param.7), kind=kLoop, calls=%fused_computation.39 | loop fusion | bytes 4194304 | tf_op jit(solution)/shard_map/slice | solution.py:191
  10.3 2.5 collective-permute-start.1
  12.8 8.1 %fusion.20 = bf16[512,2048]{1,0:T(8,128)(2,1)S(1)} fusion(bf16[512,2048]{1,0:T(8,128)(2,1)S(1)} %bitcast.29, bf16[2048,8192]{1,0:T(8,128)(2,1)} %param.8, s32[]{:T(128)S(6)} %select_n.90), kind=kOutput, calls=%fused_computation.12 | convolution fusion | flops 4296015872 | bytes 12582916 | tf_op jit(solution)/shard_map/dot_general | solution.py:227
  20.9 1.7 fusion.32
  22.6 2.1 collective-permute-start
  24.7 1.6 collective-permute-start.5
  26.6 33.5 %all-gather = s32[4,1,512]{2,1,0:T(1,128)S(1)} all-gather(s32[1,1,512]{2,1,0:T(1,128)S(1)} %bitcast.39), channel_id=1, replica_groups=mesh['groups'=2,'pool'=4,'tp'=4] {'pool'}, dimensions={0}, use_global_device_ids=true | all-gather | bytes 10240 | tf_op jit(solution)/shard_map/all_gather | solution.py:209
  60.8 9.5 %fusion.14.part_ref = f32[512,2048]{1,0:T(8,128)} fusion(bf16[512,2048]{1,0:T(8,128)(2,1)S(1)} %bitcast.30, bf16[2048,8192]{1,0:T(8,128)(2,1)} %param.8, s32[]{:T(128)S(6)} %select_n.88), kind=kOutput, calls=%fused_computation.10 | convolution fusion | flops 4294967296 | bytes 14680068 | tf_op jit(solution)/shard_map/dot_general | solution.py:227
  71.8 8.9 %shrink.2._ = f32[512,128]{1,0:T(8,128)} custom-call(bf16[512,2048]{1,0:T(8,128)(2,1)S(1)} %bitcast.31, bf16[256,2048]{1,0:T(8,128)(2,1)S(1)} %copy-done.12, bf16[512,2048]{1,0:T(8,128)(2,1)} %collective-permute-done.2.refs_2_, bf16[256,2048]{1,0:T(8,128)(2,1)} %collective-permute-done.3.refs_3_, s32[1024,128]{1,0:T(8,128)S(1)} %broadcast_in_dim.40.refs_4_.place_ref, ...), custom_call_target="tpu_custom_call" | custom-call | flops 1024 | bytes 1024 | tf_op jit(solution)/shard_map/shrink/pallas_call | solution.py:70
  80.7 2.2 copy-done.5
  82.9 3.4 %add.216.refs_6_ = bf16[256,2048]{1,0:T(8,128)(2,1)} custom-call(f32[512,2048]{1,0:T(8,128)S(1)} %copy-done.5, bf16[256,2048]{1,0:T(8,128)(2,1)} %collective-permute-done.moving_ref, f32[512,128]{1,0:T(8,128)} %shrink.2._), custom_call_target="tpu_custom_call" | custom-call | flops 256 | bytes 256 | tf_op jit(solution)/shard_map/add/pallas_call | solution.py:153
  87.2 2.2 copy-done.2
  89.4 9.2 %shrink.3._ = f32[512,128]{1,0:T(8,128)} custom-call(bf16[512,2048]{1,0:T(8,128)(2,1)S(1)} %bitcast.32, bf16[256,2048]{1,0:T(8,128)(2,1)} %collective-permute-done.6.refs_1_, bf16[512,2048]{1,0:T(8,128)(2,1)} %collective-permute-done.2.refs_2_, bf16[256,2048]{1,0:T(8,128)(2,1)} %collective-permute-done.7.refs_3_, ...), custom_call_target="tpu_custom_call" | custom-call | flops 1024 | bytes 1024 | tf_op jit(solution)/shard_map/shrink/pallas_call | solution.py:70
  98.7 2.2 copy-done.6
  100.8 3.4 %add.217._ = bf16[256,2048]{1,0:T(8,128)(2,1)} custom-call(f32[512,2048]{1,0:T(8,128)S(1)} %copy-done.6, bf16[256,2048]{1,0:T(8,128)(2,1)} %collective-permute-done.5.moving_ref, f32[512,128]{1,0:T(8,128)} %shrink.3._), custom_call_target="tpu_custom_call" | custom-call | flops 256 | bytes 256 | tf_op jit(solution)/shard_map/add/pallas_call | solution.py:153
  104.2 22.1 %all-reduce.3.cloned.1.call-done.code_ref = f32[512,128]{1,0:T(8,128)} async-done(((f32[512,128]{1,0:T(8,128)}), f32[512,128]{1,0:T(8,128)}) %all-reduce.3.cloned.1.call-update) | async-done | bytes 262160 | tf_op jit(solution)/shard_map/psum | solution.py:256
  126.3 2.2 copy-done.3
  129.5 6.4 %expand.2 = (bf16[256,2048]{1,0:T(8,128)(2,1)S(1)}, bf16[256,2048]{1,0:T(8,128)(2,1)S(1)}, bf16[256,2048]{1,0:T(8,128)(2,1)S(1)}, bf16[256,2048]{1,0:T(8,128)(2,1)}) custom-call(s32[1024,128]{1,0:T(8,128)S(1)} %broadcast_in_dim.40.refs_4_.place_ref, f32[512,128]{1,0:T(8,128)S(1)} %copy-done.15, bf16[1024,2048]{1,0:T(8,128)(2,1)S(1)} %bitcast.37, ...), custom_call_target="tpu_custom_call" | custom-call | flops 1024 | bytes 1024 | tf_op jit(solution)/shard_map/expand/pallas_call | solution.py:122
  141.6 7.0 %fusion.11.part_ref = f32[512,2048]{1,0:T(8,128)S(1)} fusion(bf16[512,2048]{1,0:T(8,128)(2,1)S(1)} %bitcast.33, bf16[2048,8192]{1,0:T(8,128)(2,1)} %param.8, s32[]{:T(128)S(6)} %select_n.86), kind=kOutput, calls=%fused_computation.9 | convolution fusion | flops 4294967296 | bytes 14680068 | tf_op jit(solution)/shard_map/dot_general | solution.py:227
  148.6 2.6 add.172._
  151.2 20.0 %collective-permute-done.4.moving_ref = bf16[256,2048]{1,0:T(8,128)(2,1)} collective-permute-done((bf16[256,2048]{1,0:T(8,128)(2,1)}, bf16[256,2048]{1,0:T(8,128)(2,1)}, u32[]{:S(2)}, u32[]{:S(2)}) %collective-permute-start.4) | collective-permute-done | bytes 1048608 | tf_op jit(solution)/shard_map/ppermute | solution.py:234
  171.2 3.4 %add.218._ = bf16[256,2048]{1,0:T(8,128)(2,1)} custom-call(f32[512,2048]{1,0:T(8,128)S(1)} %fusion.11.part_ref, bf16[256,2048]{1,0:T(8,128)(2,1)} %collective-permute-done.4.moving_ref, bf16[256,2048]{1,0:T(8,128)(2,1)} %add.172._), custom_call_target="tpu_custom_call" | custom-call | flops 256 | bytes 256 | tf_op jit(solution)/shard_map/add/pallas_call | solution.py:153
  174.6 18.6 %collective-permute-done.12.moving_ref = bf16[256,2048]{1,0:T(8,128)(2,1)} collective-permute-done((bf16[256,2048]{1,0:T(8,128)(2,1)}, bf16[256,2048]{1,0:T(8,128)(2,1)}, u32[]{:S(2)}, u32[]{:S(2)}) %collective-permute-start.12) | collective-permute-done | bytes 1048608 | tf_op jit(solution)/shard_map/ppermute | solution.py:234
  193.3 3.4 %add.219._ = bf16[256,2048]{1,0:T(8,128)(2,1)} custom-call(f32[512,2048]{1,0:T(8,128)S(1)} %fusion.11.part_ref, bf16[256,2048]{1,0:T(8,128)(2,1)} %collective-permute-done.12.moving_ref, bf16[256,2048]{1,0:T(8,128)(2,1)} %add.218._), custom_call_target="tpu_custom_call" | custom-call | flops 256 | bytes 256 | tf_op jit(solution)/shard_map/add/pallas_call | solution.py:153
  196.7 14.8 %all-reduce.5.cloned.1.call-done.code_ref = f32[512,128]{1,0:T(8,128)} async-done(((f32[512,128]{1,0:T(8,128)}), f32[512,128]{1,0:T(8,128)}) %all-reduce.5.cloned.1.call-update) | async-done | bytes 262160 | tf_op jit(solution)/shard_map/psum | solution.py:256
  211.5 2.2 copy-done.4
  214.7 6.4 %expand.3 = (bf16[256,2048]{1,0:T(8,128)(2,1)S(1)}, bf16[256,2048]{1,0:T(8,128)(2,1)S(1)}, bf16[256,2048]{1,0:T(8,128)(2,1)}, bf16[256,2048]{1,0:T(8,128)(2,1)S(1)}) custom-call(s32[1024,128]{1,0:T(8,128)S(1)} %broadcast_in_dim.41.refs_4_.place_ref, f32[512,128]{1,0:T(8,128)S(1)} %copy-done.16, bf16[1024,2048]{1,0:T(8,128)(2,1)S(1)} %bitcast.38, ...), custom_call_target="tpu_custom_call" | custom-call | flops 1024 | bytes 1024 | tf_op jit(solution)/shard_map/expand/pallas_call | solution.py:122
  228.8 7.0 %fusion.8 = f32[512,2048]{1,0:T(8,128)S(1)} fusion(bf16[512,2048]{1,0:T(8,128)(2,1)S(1)} %bitcast.34, bf16[2048,8192]{1,0:T(8,128)(2,1)} %param.8, s32[]{:T(128)S(6)} %select_n.84), kind=kOutput, calls=%fused_computation.8 | convolution fusion | flops 4294967296 | bytes 14680068 | tf_op jit(solution)/shard_map/dot_general | solution.py:227
  235.8 15.0 %collective-permute-done.13 = bf16[256,2048]{1,0:T(8,128)(2,1)} collective-permute-done((bf16[256,2048]{1,0:T(8,128)(2,1)}, bf16[256,2048]{1,0:T(8,128)(2,1)}, u32[]{:S(2)}, u32[]{:S(2)}) %collective-permute-start.13) | collective-permute-done | bytes 1048608 | tf_op jit(solution)/shard_map/ppermute | solution.py:271
  250.8 21.5 %collective-permute-done.9 = bf16[256,2048]{1,0:T(8,128)(2,1)} collective-permute-done((bf16[256,2048]{1,0:T(8,128)(2,1)}, bf16[256,2048]{1,0:T(8,128)(2,1)}, u32[]{:S(2)}, u32[]{:S(2)}) %collective-permute-start.9) | collective-permute-done | bytes 1048608 | tf_op jit(solution)/shard_map/ppermute | solution.py:271
  272.7 4.5 %fusion.26 = (bf16[256,2048]{1,0:T(8,128)(2,1)S(1)}, bf16[256,2048]{1,0:T(8,128)(2,1)S(1)}) fusion(f32[512,2048]{1,0:T(8,128)S(1)} %fusion.8, bf16[256,2048]{1,0:T(8,128)(2,1)} %collective-permute-done.9, bf16[256,2048]{1,0:T(8,128)(2,1)} %collective-permute-done.11, bf16[256,2048]{1,0:T(8,128)(2,1)S(1)} %copy-done.8, ...), kind=kLoop, calls=%fused_computation.18 | loop fusion | flops 8388608 | bytes 14680064 | tf_op jit(solution)/shard_map/convert_element_type | solution.py:273
  277.1 1.6 pad_maximum_fusion
  (79 shorter events, 19.4 us)
Async XLA Ops:
  6.5 6.3 %copy-start = (bf16[4,128,2048]{2,1,0:T(8,128)(2,1)S(1)}, bf16[4,128,2048]{2,1,0:T(8,128)(2,1)}, u32[]{:S(2)}) copy-start(bf16[4,128,2048]{2,1,0:T(8,128)(2,1)} %param.7) | copy-start | bytes 6291460
  6.5 63.8 %collective-permute-start.2 = (bf16[512,2048]{1,0:T(8,128)(2,1)}, bf16[512,2048]{1,0:T(8,128)(2,1)}, u32[]{:S(2)}, u32[]{:S(2)}) collective-permute-start(bf16[512,2048]{1,0:T(8,128)(2,1)} %bitcast.28), channel_id=1, source_target_pairs={{0,4},{4,0},{8,12},{12,8},{1,5},{5,1},{9,13},{13,9},{2,6},{6,2},{1... | collective-permute-start | bytes 6291464 | tf_op jit(solution)/shard_map/ppermute | solution.py:194
  10.3 49.8 %collective-permute-start.1 = (bf16[256,2048]{1,0:T(8,128)(2,1)}, bf16[256,2048]{1,0:T(8,128)(2,1)S(1)}, u32[]{:S(2)}, u32[]{:S(2)}) collective-permute-start(bf16[256,2048]{1,0:T(8,128)(2,1)} %bitcast.5), channel_id=1, source_target_pairs={{0,8},{4,12},{8,0},{12,4},{1,9},{5,13},{9,1},{13,5},{2,10},{6,14},... | collective-permute-start | bytes 3145736 | tf_op jit(solution)/shard_map/ppermute | solution.py:193
  12.8 47.7 %collective-permute-start.6 = (bf16[256,2048]{1,0:T(8,128)(2,1)}, bf16[256,2048]{1,0:T(8,128)(2,1)}, u32[]{:S(2)}, u32[]{:S(2)}) collective-permute-start(bf16[256,2048]{1,0:T(8,128)(2,1)} %bitcast.14), channel_id=1, source_target_pairs={{0,8},{4,12},{8,0},{12,4},{1,9},{5,13},{9,1},{13,5},{2,10},{6,14},... | collective-permute-start | bytes 3145736 | tf_op jit(solution)/shard_map/ppermute | solution.py:193
  20.9 5.4 %copy-start.20 = (s32[4,1,8]{2,1,0:T(1,128)S(1)}, s32[4,1,8]{2,1,0:T(1,128)}, u32[]{:S(2)}) copy-start(s32[4,1,8]{2,1,0:T(1,128)} %param.12) | copy-start | bytes 388
  20.9 5.4 %copy-start.21 = (s32[64]{0:T(128)S(1)}, s32[64]{0:T(128)}, u32[]{:S(2)}) copy-start(s32[64]{0:T(128)} %param.11) | copy-start | bytes 772
  20.9 5.6 %copy-start.19 = (s32[4,128]{1,0:T(4,128)S(1)}, s32[4,128]{1,0:T(4,128)}, u32[]{:S(2)}) copy-start(s32[4,128]{1,0:T(4,128)} %param.13) | copy-start | bytes 6148
  22.6 58.1 %collective-permute-start = (bf16[256,2048]{1,0:T(8,128)(2,1)}, bf16[256,2048]{1,0:T(8,128)(2,1)}, u32[]{:S(2)}, u32[]{:S(2)}) collective-permute-start(bf16[256,2048]{1,0:T(8,128)(2,1)} %get-tuple-element.27.refs_6_), channel_id=1, source_target_pairs={{0,1},{1,2},{2,3},{3,0},{4,5},{5,6},{6,7},{7,4},{8,9},{9,10},{10,1... | collective-permute-start | bytes 3145736 | tf_op jit(solution)/shard_map/ppermute | solution.py:234
  24.7 74.0 %collective-permute-start.5 = (bf16[256,2048]{1,0:T(8,128)(2,1)}, bf16[256,2048]{1,0:T(8,128)(2,1)}, u32[]{:S(2)}, u32[]{:S(2)}) collective-permute-start(bf16[256,2048]{1,0:T(8,128)(2,1)} %get-tuple-element.28), channel_id=1, source_target_pairs={{0,1},{1,2},{2,3},{3,0},{4,5},{5,6},{6,7},{7,4},{8,9},{9,10},{10,1... | collective-permute-start | bytes 3145736 | tf_op jit(solution)/shard_map/ppermute | solution.py:234
  60.1 10.2 %copy-start.11 = (bf16[256,2048]{1,0:T(8,128)(2,1)}, bf16[256,2048]{1,0:T(8,128)(2,1)S(1)}, u32[]{:S(2)}) copy-start(bf16[256,2048]{1,0:T(8,128)(2,1)S(1)} %collective-permute-done.1.refs_1_) | copy-start | bytes 3145732
  60.1 10.2 %collective-permute-start.3 = (bf16[256,2048]{1,0:T(8,128)(2,1)S(1)}, bf16[256,2048]{1,0:T(8,128)(2,1)}, u32[]{:S(2)}, u32[]{:S(2)}) collective-permute-start(bf16[256,2048]{1,0:T(8,128)(2,1)S(1)} %collective-permute-done.1.refs_1_), channel_id=1, source_target_pairs={{0,4},{4,0},{8,12},{12,8},{1,5},{5,1},{9,13},{13,9},{2,6},{6,2},{1... | collective-permute-start | bytes 3145736 | tf_op jit(solution)/shard_map/ppermute | solution.py:195
  60.5 26.5 %collective-permute-start.7 = (bf16[256,2048]{1,0:T(8,128)(2,1)}, bf16[256,2048]{1,0:T(8,128)(2,1)}, u32[]{:S(2)}, u32[]{:S(2)}) collective-permute-start(bf16[256,2048]{1,0:T(8,128)(2,1)} %collective-permute-done.6.refs_1_), channel_id=1, source_target_pairs={{0,4},{4,0},{8,12},{12,8},{1,5},{5,1},{9,13},{13,9},{2,6},{6,2},{1... | collective-permute-start | bytes 3145736 | tf_op jit(solution)/shard_map/ppermute | solution.py:195
  60.8 9.7 %copy-start.1 = (bf16[16,64,2048]{2,1,0:T(8,128)(2,1)S(1)}, bf16[16,64,2048]{2,1,0:T(8,128)(2,1)}, u32[]{:S(2)}) copy-start(bf16[16,64,2048]{2,1,0:T(8,128)(2,1)} %param.9) | copy-start | bytes 12582916
  80.7 2.2 copy-start.5
  86.3 40.0 %all-reduce.3.cloned.1.call-start = ((), (), s32[]{:S(2)}) async-start(), calls=%async_computation | async-start | bytes 524288 | tf_op jit(solution)/shard_map/psum | solution.py:256
  87.2 2.2 copy-start.2
  98.7 2.2 copy-start.6
  104.2 107.3 %all-reduce.5.cloned.1.call-start = ((), (), s32[]{:S(2)}) async-start(), calls=%async_computation.1 | async-start | bytes 524288 | tf_op jit(solution)/shard_map/psum | solution.py:256
  138.8 9.7 %collective-permute-start.8 = (bf16[256,2048]{1,0:T(8,128)(2,1)}, bf16[256,2048]{1,0:T(8,128)(2,1)}, u32[]{:S(2)}, u32[]{:S(2)}) collective-permute-start(bf16[256,2048]{1,0:T(8,128)(2,1)} %get-tuple-element.15), channel_id=1, source_target_pairs={{0,4},{4,0},{8,12},{12,8},{1,5},{5,1},{9,13},{13,9},{2,6},{6,2},{1... | collective-permute-start | bytes 3145736 | tf_op jit(solution)/shard_map/ppermute | solution.py:241
  138.8 32.3 %collective-permute-start.4 = (bf16[256,2048]{1,0:T(8,128)(2,1)}, bf16[256,2048]{1,0:T(8,128)(2,1)}, u32[]{:S(2)}, u32[]{:S(2)}) collective-permute-start(bf16[256,2048]{1,0:T(8,128)(2,1)} %add.216.refs_6_), channel_id=1, source_target_pairs={{0,1},{1,2},{2,3},{3,0},{4,5},{5,6},{6,7},{7,4},{8,9},{9,10},{10,1... | collective-permute-start | bytes 3145736 | tf_op jit(solution)/shard_map/ppermute | solution.py:234
  140.3 53.0 %collective-permute-start.12 = (bf16[256,2048]{1,0:T(8,128)(2,1)}, bf16[256,2048]{1,0:T(8,128)(2,1)}, u32[]{:S(2)}, u32[]{:S(2)}) collective-permute-start(bf16[256,2048]{1,0:T(8,128)(2,1)} %add.217._), channel_id=1, source_target_pairs={{0,1},{1,2},{2,3},{3,0},{4,5},{5,6},{6,7},{7,4},{8,9},{9,10},{10,1... | collective-permute-start | bytes 3145736 | tf_op jit(solution)/shard_map/ppermute | solution.py:234
  141.6 7.0 %copy-start.14 = (bf16[256,2048]{1,0:T(8,128)(2,1)S(1)}, bf16[256,2048]{1,0:T(8,128)(2,1)}, u32[]{:S(2)}) copy-start(bf16[256,2048]{1,0:T(8,128)(2,1)} %copy-done.13) | copy-start | bytes 3145732
  214.7 7.5 %copy-start.18 = (bf16[256,2048]{1,0:T(8,128)(2,1)S(1)}, bf16[256,2048]{1,0:T(8,128)(2,1)}, u32[]{:S(2)}) copy-start(bf16[256,2048]{1,0:T(8,128)(2,1)} %copy-done.17) | copy-start | bytes 3145732
  222.1 4.7 %collective-permute-start.15 = (bf16[256,2048]{1,0:T(8,128)(2,1)S(1)}, bf16[256,2048]{1,0:T(8,128)(2,1)S(1)}, u32[]{:S(2)}, u32[]{:S(2)}) collective-permute-start(bf16[256,2048]{1,0:T(8,128)(2,1)S(1)} %get-tuple-element.22), channel_id=1, source_target_pairs={{0,4},{4,0},{8,12},{12,8},{1,5},{5,1},{9,13},{13,9},{2,6},{6,2},{1... | collective-permute-start | bytes 3145736 | tf_op jit(solution)/shard_map/ppermute | solution.py:241
  222.1 6.1 %collective-permute-start.10 = (bf16[256,2048]{1,0:T(8,128)(2,1)S(1)}, bf16[256,2048]{1,0:T(8,128)(2,1)S(1)}, u32[]{:S(2)}, u32[]{:S(2)}) collective-permute-start(bf16[256,2048]{1,0:T(8,128)(2,1)S(1)} %copy-done.18), channel_id=1, source_target_pairs={{0,4},{4,0},{8,12},{12,8},{1,5},{5,1},{9,13},{13,9},{2,6},{6,2},{1... | collective-permute-start | bytes 3145736 | tf_op jit(solution)/shard_map/ppermute | solution.py:241
  222.6 28.1 %collective-permute-start.13 = (bf16[256,2048]{1,0:T(8,128)(2,1)}, bf16[256,2048]{1,0:T(8,128)(2,1)}, u32[]{:S(2)}, u32[]{:S(2)}) collective-permute-start(bf16[256,2048]{1,0:T(8,128)(2,1)} %add.219._), channel_id=1, source_target_pairs={{0,1},{1,2},{2,3},{3,0},{4,5},{5,6},{6,7},{7,4},{8,9},{9,10},{10,1... | collective-permute-start | bytes 3145736 | tf_op jit(solution)/shard_map/ppermute | solution.py:271
  224.1 48.2 %collective-permute-start.9 = (bf16[256,2048]{1,0:T(8,128)(2,1)}, bf16[256,2048]{1,0:T(8,128)(2,1)}, u32[]{:S(2)}, u32[]{:S(2)}) collective-permute-start(bf16[256,2048]{1,0:T(8,128)(2,1)} %add.218._), channel_id=1, source_target_pairs={{0,1},{1,2},{2,3},{3,0},{4,5},{5,6},{6,7},{7,4},{8,9},{9,10},{10,1... | collective-permute-start | bytes 3145736 | tf_op jit(solution)/shard_map/ppermute | solution.py:271
  225.4 46.9 %collective-permute-start.11 = (bf16[256,2048]{1,0:T(8,128)(2,1)}, bf16[256,2048]{1,0:T(8,128)(2,1)}, u32[]{:S(2)}, u32[]{:S(2)}) collective-permute-start(bf16[256,2048]{1,0:T(8,128)(2,1)} %add.172._), channel_id=1, source_target_pairs={{0,8},{4,12},{8,0},{12,4},{1,9},{5,13},{9,1},{13,5},{2,10},{6,14},... | collective-permute-start | bytes 3145736 | tf_op jit(solution)/shard_map/ppermute | solution.py:244
  226.8 9.0 %collective-permute-start.14 = (bf16[256,2048]{1,0:T(8,128)(2,1)}, bf16[256,2048]{1,0:T(8,128)(2,1)}, u32[]{:S(2)}, u32[]{:S(2)}) collective-permute-start(bf16[256,2048]{1,0:T(8,128)(2,1)} %get-tuple-element.20), channel_id=1, source_target_pairs={{0,4},{4,0},{8,12},{12,8},{1,5},{5,1},{9,13},{13,9},{2,6},{6,2},{1... | collective-permute-start | bytes 3145736 | tf_op jit(solution)/shard_map/ppermute | solution.py:241
  228.2 44.5 %collective-permute-start.16 = (bf16[256,2048]{1,0:T(8,128)(2,1)}, bf16[256,2048]{1,0:T(8,128)(2,1)}, u32[]{:S(2)}, u32[]{:S(2)}) collective-permute-start(bf16[256,2048]{1,0:T(8,128)(2,1)} %add.179), channel_id=1, source_target_pairs={{0,8},{4,12},{8,0},{12,4},{1,9},{5,13},{9,1},{13,5},{2,10},{6,14},... | collective-permute-start | bytes 3145736 | tf_op jit(solution)/shard_map/ppermute | solution.py:244
  228.8 43.9 %copy-start.8 = (bf16[256,2048]{1,0:T(8,128)(2,1)S(1)}, bf16[256,2048]{1,0:T(8,128)(2,1)}, u32[]{:S(2)}) copy-start(bf16[256,2048]{1,0:T(8,128)(2,1)} %copy-done.7) | copy-start | bytes 3145732
  228.8 43.9 %copy-start.10 = (bf16[256,2048]{1,0:T(8,128)(2,1)S(1)}, bf16[256,2048]{1,0:T(8,128)(2,1)}, u32[]{:S(2)}) copy-start(bf16[256,2048]{1,0:T(8,128)(2,1)} %copy-done.9) | copy-start | bytes 3145732
  (9 other events, 11.5 us)
Sparse Core Ops, SparseCore 0:
  89.4 36.8 all-reduce.2
  141.7 69.7 all-reduce.4

commit v3 on v1

--- a/solution.py
+++ b/solution.py
@@ -133,9 +133,9 @@
     steps_count, rows_count, feature_shard = inputs.shape
     stored, rank = shrink_store.shape[:2]
     slot_count = requests.shape[2]
-    pool_size, tp_size = lax.axis_size("pool"), lax.axis_size("tp")
+    pool_size = lax.axis_size("pool")
     chips = pool_size // 2
-    my_pool, my_tp = lax.axis_index("pool"), lax.axis_index("tp")
+    my_pool = lax.axis_index("pool")
     my_chip, my_core = my_pool // 2, my_pool % 2
     all_rows = steps_count * rows_count
     flat = inputs.reshape(all_rows, feature_shard)
@@ -144,13 +144,6 @@
 
     swap = [(p, p ^ 1) for p in range(pool_size)]
     shift = lambda k: [(p, (p // 2 + k) % chips * 2 + p % 2) for p in range(pool_size)]
-    around = [(i, (i + 1) % tp_size) for i in range(tp_size)]
-
-    per_half = all_rows // HALVES
-    halves = [flat[h * per_half : (h + 1) * per_half] for h in range(HALVES)]
-
-    mine = [[half] + [lax.ppermute(half, "pool", shift(k)) for k in range(1, chips)] for half in halves]
-    theirs = [[lax.ppermute(part, "pool", swap) for part in group] for group in mine]
 
     ids = jnp.arange(owner_map.shape[0], dtype=jnp.int32)
     positions = jnp.sum(
@@ -161,9 +154,16 @@
         jnp.where(row_slot[:, :, None] == slots, positions[:, None, :], 0), axis=-1
     )
     every = lax.all_gather(row_position.reshape(1, all_rows), "pool", axis=0, tiled=True)
+    every, flat_sent = lax.optimization_barrier((every, flat))
     every = every - my_pool * stored
 
-    def places(h):
+    per_half = all_rows // HALVES
+    halves = [flat_sent[h * per_half : (h + 1) * per_half] for h in range(HALVES)]
+
+    mine = [[half] + [lax.ppermute(half, "pool", shift(k)) for k in range(1, chips)] for half in halves]
+    theirs = [[lax.ppermute(part, "pool", swap) for part in group] for group in mine]
+
+    def places(h, every):
         found = []
         for core in (my_core, 1 - my_core):
             for k in range(chips):
@@ -173,31 +173,29 @@
                 )
         return jnp.broadcast_to(jnp.concatenate(found)[:, None], (pool_size * per_half, LANES))
 
-    def base_part(back):
-        target = (my_tp - back + tp_size) % tp_size
-        columns = lax.dynamic_slice(
-            out_weight, (0, target * feature_shard), (out_weight.shape[0], feature_shard)
-        )
-        return jnp.dot(flat, columns, preferred_element_type=jnp.float32)
+    def partial_of(rows):
+        return lax.dot_general(
+            out_weight, rows, (((0,), (1,)), ((), ())), preferred_element_type=jnp.float32
+        ).astype(jnp.bfloat16)
+
+    def base_of(partial):
+        return lax.psum_scatter(partial, "tp", scatter_dimension=0, tiled=True)
 
     cut = lambda array, s: array[s * rows_count : (s + 1) * rows_count]
-    part = base_part(1)
-    moving = [cut(part, s).astype(jnp.bfloat16) for s in range(steps_count)]
-    for back in range(2, tp_size + 1):
-        part = base_part(back)
-        moving = [
-            cut(part, s) + lax.ppermute(moving[s], "tp", around).astype(jnp.float32)
-            for s in range(steps_count)
-        ]
-        if back < tp_size:
-            moving = [m.astype(jnp.bfloat16) for m in moving]
+    early = [partial_of(cut(flat, s)) for s in range(steps_count // HALVES)]
+    bases = [base_of(partial) for partial in early]
+    every, *_ = lax.optimization_barrier((every, *early))
+    place = [places(h, every) for h in range(HALVES)]
+    codes = [shrink(mine[h] + theirs[h], place[h], shrink_flat, rank) for h in range(HALVES)]
+    later, *codes = lax.optimization_barrier((flat[steps_count // HALVES * rows_count :], *codes))
+    partial, bases, codes = lax.optimization_barrier((partial_of(later), bases, codes))
+    codes = lax.psum(codes, "tp")
+    bases = [base.T for base in [*bases, base_of(partial)]]
+    moving = jnp.concatenate(bases, axis=0).astype(jnp.float32)
 
     updates = []
     for h in range(HALVES):
-        place = places(h)
-        codes = shrink(mine[h] + theirs[h], place, shrink_flat, rank)
-        codes = lax.psum(codes, "tp")
-        terms = expand(codes, place, expand_flat, rank, pool_size)
+        terms = expand(codes[h], place[h], expand_flat, rank, pool_size)
         total = None
         for k in range(chips):
             joined = terms[k] + lax.ppermute(terms[chips + k], "pool", swap)
@@ -206,15 +204,8 @@
             total = joined if total is None else total + joined
         updates.append(total)
 
-    per = steps_count // HALVES
-    rows_out = [
-        (
-            moving[s]
-            + adapter_scale * cut(updates[s // per], s % per).astype(jnp.float32)
-        ).astype(jnp.bfloat16)
-        for s in range(steps_count)
-    ]
-    return jnp.stack(rows_out, axis=0)
+    update = jnp.concatenate(updates, axis=0).astype(jnp.float32)
+    return (moving + adapter_scale * update).astype(jnp.bfloat16).reshape(inputs.shape)
 
 
 def solution(mesh):

time: 257 us -> 250 us (0.973)
  matrix products: 32.8 us -> 50.2 us
  starting transfers between devices: 24.2 us -> 7.03 us
  waiting for transfers between devices: 134 us -> 128 us
    ppermute x12 -> x0, waiting for transfers between devices: 60.8 us -> none  [body(): lax.ppermute(moving[s], 'tp', around).astype(jnp.float32)]
    ppermute x2, waiting for transfers between devices: 9.17 us -> 44.1 us  [body(): joined = lax.ppermute(joined, 'pool', shift(chips - k))]
    dot_general x4 -> x3, matrix products: 32.8 us -> 50.2 us  [partial_of(): lax.dot_general(out_weight, rows, (((0,), (1,)), ((), ())), preferred_ele...]
    ppermute x12 -> x0, starting transfers between devices: 17.1 us -> none  [body(): lax.ppermute(moving[s], 'tp', around).astype(jnp.float32)]
    reduce_scatter x0 -> x3, waiting for transfers between devices: none -> 14.8 us  [base_of(): return lax.psum_scatter(partial, 'tp', scatter_dimension=0, tiled=True)]
    psum x1, waiting for transfers between devices: 31.5 us -> 39.7 us  [body(): codes = lax.psum(codes, 'tp')]
    ppermute x2, waiting for transfers between devices: 32.7 us -> 28.6 us  [body(): lax.ppermute(half, 'pool', shift(k))]
    another operation x2 -> x0, other arithmetic: 2.68 us -> none  [body(): return jnp.stack(rows_out, axis=0)]
  transfers between devices with their start and end apart: 25 -> 16, of which waited for: 12 -> 7; matrix products, arithmetic and copies ran while one was open for 15% -> 16% of each run, Pallas kernels for 12% -> 12%
where the time goes in v3:
time: 250 us
  waiting for transfers between devices  128 us (51%)
  matrix products  50.2 us (20%)
  Pallas kernels  30 us (12%)
  between operations  13.3 us (5%)
  local copies, waits for them, and re-layouts  11.1 us (4%)
  starting transfers between devices  7.03 us (3%)
  blocking collectives  6.1 us (2%)
  other arithmetic  4.61 us (2%)
    dot_general x3, matrix products, partial_of(): lax.dot_general(out_weight, rows, (((0,), (1,)), ((), ())), preferred_ele...  50.2 us
    ppermute x2, waiting for transfers between devices, body(): joined = lax.ppermute(joined, 'pool', shift(chips - k))  44.1 us
    psum x1, waiting for transfers between devices, body(): codes = lax.psum(codes, 'tp')  39.7 us
    ppermute x2, waiting for transfers between devices, body(): lax.ppermute(half, 'pool', shift(k))  28.6 us
    pallas_call x2, Pallas kernels, shrink(): pl.pallas_call(functools.partial(shrink_kernel, count, rank), grid=(width...  18.4 us
    reduce_scatter x3, waiting for transfers between devices, base_of(): return lax.psum_scatter(partial, 'tp', scatter_dimension=0, tiled=True)  14.8 us
    pallas_call x2, Pallas kernels, expand(): pl.pallas_call(functools.partial(expand_kernel, count, rank), grid=(featu...  11.6 us
    unnamed x23, local copies, waits for them, and re-layouts  6.58 us
  transfers between devices with their start and end apart: 16, of which 7 were waited for; matrix products, arithmetic and copies ran while one was open for 16% of the time, Pallas kernels for 12%

profile of v3, /device:TPU:0, one launch (start us, length us, event | category | flops | bytes accessed | tf_op | source)
XLA Modules:
  0.0 250.1 jit_solution(3200943891767882410)
XLA Ops:
  6.5 16.6 %convolution_convert_fusion.1 = bf16[8192,128]{0,1:T(8,128)(2,1)} fusion(bf16[2048,8192]{1,0:T(8,128)(2,1)} %param.8, bf16[4,128,2048]{2,1,0:T(8,128)(2,1)} %param.7), kind=kOutput, calls=%fused_computation.2 | convolution fusion | flops 4296015872 | bytes 36175872 | tf_op jit(solution)/shard_map/dot_general | solution.py:177
  23.2 0.2 select_reduce_fusion.1
  23.5 6.1 %all-gather = s32[4,1,512]{2,1,0:T(1,128)S(1)} all-gather(s32[1,1,512]{2,1,0:T(1,128)S(1)} %bitcast.43), channel_id=1, replica_groups=mesh['groups'=2,'pool'=4,'tp'=4] {'pool'}, dimensions={0}, use_global_device_ids=true | all-gather | bytes 10240 | tf_op jit(solution)/shard_map/all_gather | solution.py:156
  29.6 1.8 fusion.5
  31.4 2.1 collective-permute-start.3
  33.6 16.7 %convolution_convert_fusion.2 = bf16[8192,128]{0,1:T(8,128)(2,1)} fusion(bf16[2048,8192]{1,0:T(8,128)(2,1)} %param.8, bf16[4,128,2048]{2,1,0:T(8,128)(2,1)} %param.7), kind=kOutput, calls=%fused_computation.3 | convolution fusion | flops 4296015872 | bytes 36175872 | tf_op jit(solution)/shard_map/dot_general | solution.py:177
  50.3 0.2 all-reduce.3.cloned.1.call-start
  50.6 6.8 %collective-permute-done.3.refs_1_ = bf16[256,2048]{1,0:T(8,128)(2,1)S(1)} collective-permute-done((bf16[256,2048]{1,0:T(8,128)(2,1)S(1)}, bf16[256,2048]{1,0:T(8,128)(2,1)S(1)}, u32[]{:S(2)}, u32[]{:S(2)}) %collective-permute-start.3) | collective-permute-done | bytes 1048608 | tf_op jit(solution)/shard_map/ppermute | solution.py:163
  57.4 0.5 collective-permute-start.1
  58.0 21.7 %collective-permute-done.refs_1_ = bf16[256,2048]{1,0:T(8,128)(2,1)} collective-permute-done((bf16[256,2048]{1,0:T(8,128)(2,1)S(1)}, bf16[256,2048]{1,0:T(8,128)(2,1)}, u32[]{:S(2)}, u32[]{:S(2)}) %collective-permute-start) | collective-permute-done | bytes 1048608 | tf_op jit(solution)/shard_map/ppermute | solution.py:163
  79.7 2.3 slice.24
  82.3 2.2 copy-done
  84.5 1.2 copy-done.5
  85.7 9.1 %shrink.3 = f32[512,128]{1,0:T(8,128)} custom-call(bf16[256,2048]{1,0:T(8,128)(2,1)S(1)} %get-tuple-element.45.refs_0_, bf16[256,2048]{1,0:T(8,128)(2,1)S(1)} %copy-done.5, bf16[256,2048]{1,0:T(8,128)(2,1)} %collective-permute-done.4.refs_2_, bf16[256,2048]{1,0:T(8,128)(2,1)} %collective-permute-done.5.refs_3_, ...), custom_call_target="tpu_custom_call" | custom-call | flops 4294967296 | bytes 8388608 | tf_op jit(solution)/shard_map/shrink/pallas_call | solution.py:66
  94.8 0.2 broadcast_in_dim.40.refs_4_.place_ref
  95.0 9.3 %shrink.2 = f32[512,128]{1,0:T(8,128)} custom-call(bf16[256,2048]{1,0:T(8,128)(2,1)S(1)} %get-tuple-element.46.refs_0_, bf16[256,2048]{1,0:T(8,128)(2,1)} %collective-permute-done.refs_1_, bf16[256,2048]{1,0:T(8,128)(2,1)} %collective-permute-done.1.refs_2_, bf16[256,2048]{1,0:T(8,128)(2,1)} %collective-permute-done.2.refs_3_, ...), custom_call_target="tpu_custom_call" | custom-call | flops 4294967296 | bytes 8388608 | tf_op jit(solution)/shard_map/shrink/pallas_call | solution.py:66
  104.3 16.9 %fusion = bf16[8192,256]{0,1:T(8,128)(2,1)} fusion(bf16[256,2048]{1,0:T(8,128)(2,1)} %bitcast.38, bf16[2048,8192]{1,0:T(8,128)(2,1)} %param.8), kind=kOutput, calls=%fused_computation.1 | convolution fusion | flops 8592031744 | bytes 38797312 | tf_op jit(solution)/shard_map/dot_general | solution.py:177
  121.3 0.5 reduce-scatter.8.cloned.1.call-update
  121.8 39.7 %all-reduce.3.cloned.1.call-done = (f32[512,128]{1,0:T(8,128)}, f32[512,128]{1,0:T(8,128)}) async-done(((f32[512,128]{1,0:T(8,128)}, f32[512,128]{1,0:T(8,128)}), (f32[512,128]{1,0:T(8,128)}, f32[512,128]{1,0:T(8,128)})) %all-reduce.3.cloned.1.call-update) | async-done | bytes 524304 | tf_op jit(solution)/shard_map/psum | solution.py:192
  161.5 2.2 copy-done.2
  163.7 0.9 copy-done.7
  164.6 5.8 %expand.3 = (bf16[256,2048]{1,0:T(8,128)(2,1)S(1)}, bf16[256,2048]{1,0:T(8,128)(2,1)S(1)}, bf16[256,2048]{1,0:T(8,128)(2,1)S(1)}, bf16[256,2048]{1,0:T(8,128)(2,1)S(1)}) custom-call(s32[1024,128]{1,0:T(8,128)S(1)} %broadcast_in_dim.41.refs_4_.place_ref, f32[512,128]{1,0:T(8,128)S(1)} %copy-done.7, bf16[1024,2048]{1,0:T(8,128)(2,1)S(1)} %bitcast.35), custom_call_target="tpu_custom_call" | custom-call | flops 4294967296 | bytes 8388608 | tf_op jit(solution)/shard_map/expand/pallas_call | solution.py:114
  170.5 5.8 %expand.2 = (bf16[256,2048]{1,0:T(8,128)(2,1)S(1)}, bf16[256,2048]{1,0:T(8,128)(2,1)S(1)}, bf16[256,2048]{1,0:T(8,128)(2,1)S(1)}, bf16[256,2048]{1,0:T(8,128)(2,1)S(1)}) custom-call(s32[1024,128]{1,0:T(8,128)S(1)} %broadcast_in_dim.40.refs_4_.place_ref, f32[512,128]{1,0:T(8,128)S(1)} %copy-done.6, bf16[1024,2048]{1,0:T(8,128)(2,1)S(1)} %bitcast.36), custom_call_target="tpu_custom_call" | custom-call | flops 4294967296 | bytes 8388608 | tf_op jit(solution)/shard_map/expand/pallas_call | solution.py:114
  176.3 0.5 collective-permute-start.7
  176.9 0.4 add.114
  177.3 1.6 collective-permute-start.11
  179.2 0.4 add.111
  179.5 1.6 collective-permute-start.8
  181.1 22.3 %collective-permute-done.11 = bf16[256,2048]{1,0:T(8,128)(2,1)S(1)} collective-permute-done((bf16[256,2048]{1,0:T(8,128)(2,1)S(1)}, bf16[256,2048]{1,0:T(8,128)(2,1)S(1)}, u32[]{:S(2)}, u32[]{:S(2)}) %collective-permute-start.11) | collective-permute-done | bytes 1048608 | tf_op jit(solution)/shard_map/ppermute | solution.py:203
  203.6 21.8 %collective-permute-done.8 = bf16[256,2048]{1,0:T(8,128)(2,1)S(1)} collective-permute-done((bf16[256,2048]{1,0:T(8,128)(2,1)S(1)}, bf16[256,2048]{1,0:T(8,128)(2,1)S(1)}, u32[]{:S(2)}, u32[]{:S(2)}) %collective-permute-start.8) | collective-permute-done | bytes 1048608 | tf_op jit(solution)/shard_map/ppermute | solution.py:203
  225.5 14.8 %reduce-scatter.8.cloned.1.call-done = bf16[2048,256]{0,1:T(8,128)(2,1)} async-done(((bf16[8192,256]{0,1:T(8,128)(2,1)}), bf16[2048,256]{0,1:T(8,128)(2,1)}) %reduce-scatter.8.cloned.1.call-update) | async-done | bytes 1048592 | tf_op jit(solution)/shard_map/reduce_scatter | solution.py:182
  240.4 3.2 %add_convert_fusion = bf16[512,2048]{1,0:T(8,128)(2,1)} fusion(bf16[256,2048]{1,0:T(8,128)(2,1)} %bitcast.39, bf16[128,2048]{1,0:T(8,128)(2,1)} %bitcast.40, bf16[128,2048]{1,0:T(8,128)(2,1)} %bitcast.41, bf16[256,2048]{1,0:T(8,128)(2,1)S(1)} %add_add_fusion, bf16[256,2048]{1,0:T(8,128)(2,1)S(1)} %add_add_fusion.1), kind=kLoop, calls=%fused_computation.4 | loop fusion | flops 13631488 | bytes 6291456 | tf_op jit(solution)/shard_map/convert_element_type | solution.py:208
  (50 shorter events, 1.4 us)
Async XLA Ops:
  6.5 16.7 %copy-start.9 = (s32[4,1,8]{2,1,0:T(1,128)S(1)}, s32[4,1,8]{2,1,0:T(1,128)}, u32[]{:S(2)}) copy-start(s32[4,1,8]{2,1,0:T(1,128)} %param.12) | copy-start | bytes 388
  6.5 16.7 %copy-start.10 = (s32[64]{0:T(128)S(1)}, s32[64]{0:T(128)}, u32[]{:S(2)}) copy-start(s32[64]{0:T(128)} %param.11) | copy-start | bytes 772
  6.5 16.9 %copy-start.8 = (s32[4,128]{1,0:T(4,128)S(1)}, s32[4,128]{1,0:T(4,128)}, u32[]{:S(2)}) copy-start(s32[4,128]{1,0:T(4,128)} %param.13) | copy-start | bytes 6148
  6.5 114.6 %reduce-scatter.6.cloned.1.call-start = ((), (), s32[]{:S(2)}) async-start(), calls=%async_computation.4 | async-start | bytes 2621440 | tf_op jit(solution)/shard_map/reduce_scatter | solution.py:182
  23.2 98.0 %reduce-scatter.4.cloned.1.call-start = ((), (), s32[]{:S(2)}) async-start(), calls=%async_computation.3 | async-start | bytes 2621440 | tf_op jit(solution)/shard_map/reduce_scatter | solution.py:182
  31.4 26.0 %collective-permute-start.3 = (bf16[256,2048]{1,0:T(8,128)(2,1)S(1)}, bf16[256,2048]{1,0:T(8,128)(2,1)S(1)}, u32[]{:S(2)}, u32[]{:S(2)}) collective-permute-start(bf16[256,2048]{1,0:T(8,128)(2,1)S(1)} %get-tuple-element.45.refs_0_), channel_id=1, source_target_pairs={{0,8},{4,12},{8,0},{12,4},{1,9},{5,13},{9,1},{13,5},{2,10},{6,14},... | collective-permute-start | bytes 3145736 | tf_op jit(solution)/shard_map/ppermute | solution.py:163
  33.5 46.2 %collective-permute-start = (bf16[256,2048]{1,0:T(8,128)(2,1)S(1)}, bf16[256,2048]{1,0:T(8,128)(2,1)}, u32[]{:S(2)}, u32[]{:S(2)}) collective-permute-start(bf16[256,2048]{1,0:T(8,128)(2,1)S(1)} %get-tuple-element.46.refs_0_), channel_id=1, source_target_pairs={{0,8},{4,12},{8,0},{12,4},{1,9},{5,13},{9,1},{13,5},{2,10},{6,14},... | collective-permute-start | bytes 3145736 | tf_op jit(solution)/shard_map/ppermute | solution.py:163
  50.3 111.2 %all-reduce.3.cloned.1.call-start = ((), (), s32[]{:S(2)}) async-start(), calls=%async_computation.6 | async-start | bytes 1048576 | tf_op jit(solution)/shard_map/psum | solution.py:192
  50.5 31.5 %collective-permute-start.4 = (bf16[256,2048]{1,0:T(8,128)(2,1)S(1)}, bf16[256,2048]{1,0:T(8,128)(2,1)}, u32[]{:S(2)}, u32[]{:S(2)}) collective-permute-start(bf16[256,2048]{1,0:T(8,128)(2,1)S(1)} %get-tuple-element.45.refs_0_), channel_id=1, source_target_pairs={{0,4},{4,0},{8,12},{12,8},{1,5},{5,1},{9,13},{13,9},{2,6},{6,2},{1... | collective-permute-start | bytes 3145736 | tf_op jit(solution)/shard_map/ppermute | solution.py:164
  57.4 24.6 %copy-start.4 = (bf16[256,2048]{1,0:T(8,128)(2,1)}, bf16[256,2048]{1,0:T(8,128)(2,1)S(1)}, u32[]{:S(2)}) copy-start(bf16[256,2048]{1,0:T(8,128)(2,1)S(1)} %collective-permute-done.3.refs_1_) | copy-start | bytes 3145732
  57.4 24.6 %collective-permute-start.5 = (bf16[256,2048]{1,0:T(8,128)(2,1)S(1)}, bf16[256,2048]{1,0:T(8,128)(2,1)}, u32[]{:S(2)}, u32[]{:S(2)}) collective-permute-start(bf16[256,2048]{1,0:T(8,128)(2,1)S(1)} %collective-permute-done.3.refs_1_), channel_id=1, source_target_pairs={{0,4},{4,0},{8,12},{12,8},{1,5},{5,1},{9,13},{13,9},{2,6},{6,2},{1... | collective-permute-start | bytes 3145736 | tf_op jit(solution)/shard_map/ppermute | solution.py:164
  57.4 37.3 %collective-permute-start.1 = (bf16[256,2048]{1,0:T(8,128)(2,1)S(1)}, bf16[256,2048]{1,0:T(8,128)(2,1)}, u32[]{:S(2)}, u32[]{:S(2)}) collective-permute-start(bf16[256,2048]{1,0:T(8,128)(2,1)S(1)} %get-tuple-element.46.refs_0_), channel_id=1, source_target_pairs={{0,4},{4,0},{8,12},{12,8},{1,5},{5,1},{9,13},{13,9},{2,6},{6,2},{1... | collective-permute-start | bytes 3145736 | tf_op jit(solution)/shard_map/ppermute | solution.py:164
  79.7 15.1 %collective-permute-start.2 = (bf16[256,2048]{1,0:T(8,128)(2,1)}, bf16[256,2048]{1,0:T(8,128)(2,1)}, u32[]{:S(2)}, u32[]{:S(2)}) collective-permute-start(bf16[256,2048]{1,0:T(8,128)(2,1)} %collective-permute-done.refs_1_), channel_id=1, source_target_pairs={{0,4},{4,0},{8,12},{12,8},{1,5},{5,1},{9,13},{13,9},{2,6},{6,2},{1... | collective-permute-start | bytes 3145736 | tf_op jit(solution)/shard_map/ppermute | solution.py:164
  82.3 2.2 copy-start
  84.5 1.2 copy-start.5
  85.7 9.3 %copy-start.1 = (bf16[16,64,2048]{2,1,0:T(8,128)(2,1)S(1)}, bf16[16,64,2048]{2,1,0:T(8,128)(2,1)}, u32[]{:S(2)}) copy-start(bf16[16,64,2048]{2,1,0:T(8,128)(2,1)} %param.9) | copy-start | bytes 12582916
  121.2 119.2 %reduce-scatter.8.cloned.1.call-start = ((), (), s32[]{:S(2)}) async-start(), calls=%async_computation.5 | async-start | bytes 5242880 | tf_op jit(solution)/shard_map/reduce_scatter | solution.py:182
  161.5 2.2 copy-start.2
  163.7 0.9 copy-start.7
  164.6 5.9 %copy-start.3 = (bf16[16,64,2048]{2,1,0:T(8,128)(2,1)S(1)}, bf16[16,64,2048]{2,1,0:T(8,128)(2,1)}, u32[]{:S(2)}) copy-start(bf16[16,64,2048]{2,1,0:T(8,128)(2,1)} %param.10) | copy-start | bytes 12582916
  164.6 5.9 %copy-start.6 = (f32[512,128]{1,0:T(8,128)S(1)}, f32[512,128]{1,0:T(8,128)}, u32[]{:S(2)}) copy-start(f32[512,128]{1,0:T(8,128)} %get-tuple-element.44.code_ref) | copy-start | bytes 786436
  170.4 6.5 %collective-permute-start.10 = (bf16[256,2048]{1,0:T(8,128)(2,1)S(1)}, bf16[256,2048]{1,0:T(8,128)(2,1)S(1)}, u32[]{:S(2)}, u32[]{:S(2)}) collective-permute-start(bf16[256,2048]{1,0:T(8,128)(2,1)S(1)} %get-tuple-element.42), channel_id=1, source_target_pairs={{0,4},{4,0},{8,12},{12,8},{1,5},{5,1},{9,13},{13,9},{2,6},{6,2},{1... | collective-permute-start | bytes 3145736 | tf_op jit(solution)/shard_map/ppermute | solution.py:201
  176.3 2.8 %collective-permute-start.7 = (bf16[256,2048]{1,0:T(8,128)(2,1)S(1)}, bf16[256,2048]{1,0:T(8,128)(2,1)S(1)}, u32[]{:S(2)}, u32[]{:S(2)}) collective-permute-start(bf16[256,2048]{1,0:T(8,128)(2,1)S(1)} %get-tuple-element.37), channel_id=1, source_target_pairs={{0,4},{4,0},{8,12},{12,8},{1,5},{5,1},{9,13},{13,9},{2,6},{6,2},{1... | collective-permute-start | bytes 3145736 | tf_op jit(solution)/shard_map/ppermute | solution.py:201
  176.9 4.2 %collective-permute-start.9 = (bf16[256,2048]{1,0:T(8,128)(2,1)S(1)}, bf16[256,2048]{1,0:T(8,128)(2,1)S(1)}, u32[]{:S(2)}, u32[]{:S(2)}) collective-permute-start(bf16[256,2048]{1,0:T(8,128)(2,1)S(1)} %get-tuple-element.40), channel_id=1, source_target_pairs={{0,4},{4,0},{8,12},{12,8},{1,5},{5,1},{9,13},{13,9},{2,6},{6,2},{1... | collective-permute-start | bytes 3145736 | tf_op jit(solution)/shard_map/ppermute | solution.py:201
  177.3 26.0 %collective-permute-start.11 = (bf16[256,2048]{1,0:T(8,128)(2,1)S(1)}, bf16[256,2048]{1,0:T(8,128)(2,1)S(1)}, u32[]{:S(2)}, u32[]{:S(2)}) collective-permute-start(bf16[256,2048]{1,0:T(8,128)(2,1)S(1)} %add.114), channel_id=1, source_target_pairs={{0,8},{4,12},{8,0},{12,4},{1,9},{5,13},{9,1},{13,5},{2,10},{6,14},... | collective-permute-start | bytes 3145736 | tf_op jit(solution)/shard_map/ppermute | solution.py:203
  178.9 24.7 %collective-permute-start.6 = (bf16[256,2048]{1,0:T(8,128)(2,1)S(1)}, bf16[256,2048]{1,0:T(8,128)(2,1)S(1)}, u32[]{:S(2)}, u32[]{:S(2)}) collective-permute-start(bf16[256,2048]{1,0:T(8,128)(2,1)S(1)} %get-tuple-element.35), channel_id=1, source_target_pairs={{0,4},{4,0},{8,12},{12,8},{1,5},{5,1},{9,13},{13,9},{2,6},{6,2},{1... | collective-permute-start | bytes 3145736 | tf_op jit(solution)/shard_map/ppermute | solution.py:201
  179.5 45.8 %collective-permute-start.8 = (bf16[256,2048]{1,0:T(8,128)(2,1)S(1)}, bf16[256,2048]{1,0:T(8,128)(2,1)S(1)}, u32[]{:S(2)}, u32[]{:S(2)}) collective-permute-start(bf16[256,2048]{1,0:T(8,128)(2,1)S(1)} %add.111), channel_id=1, source_target_pairs={{0,8},{4,12},{8,0},{12,4},{1,9},{5,13},{9,1},{13,5},{2,10},{6,14},... | collective-permute-start | bytes 3145736 | tf_op jit(solution)/shard_map/ppermute | solution.py:203
Sparse Core Ops, SparseCore 0:
  23.3 46.5 reduce-scatter.5
  72.3 43.1 reduce-scatter.3
  121.3 40.1 all-reduce.2
  163.6 76.6 reduce-scatter.7

commit v4 on v3

--- a/solution.py
+++ b/solution.py
@@ -133,10 +133,9 @@
     steps_count, rows_count, feature_shard = inputs.shape
     stored, rank = shrink_store.shape[:2]
     slot_count = requests.shape[2]
-    pool_size = lax.axis_size("pool")
+    pool_size, tp_size = lax.axis_size("pool"), lax.axis_size("tp")
     chips = pool_size // 2
-    my_pool = lax.axis_index("pool")
-    my_chip, my_core = my_pool // 2, my_pool % 2
+    my_pool, my_tp = lax.axis_index("pool"), lax.axis_index("tp")
     all_rows = steps_count * rows_count
     flat = inputs.reshape(all_rows, feature_shard)
     shrink_flat = shrink_store.reshape(stored * rank, feature_shard)
@@ -153,25 +152,39 @@
     row_position = jnp.sum(
         jnp.where(row_slot[:, :, None] == slots, positions[:, None, :], 0), axis=-1
     )
-    every = lax.all_gather(row_position.reshape(1, all_rows), "pool", axis=0, tiled=True)
-    every, flat_sent = lax.optimization_barrier((every, flat))
+    own = row_position.reshape(1, all_rows)
+    same_core = jnp.concatenate(
+        [own] + [lax.ppermute(own, "pool", shift(k)) for k in range(1, chips)], axis=0
+    )
+    every = jnp.concatenate([same_core, lax.ppermute(same_core, "pool", swap)], axis=0)
     every = every - my_pool * stored
 
     per_half = all_rows // HALVES
-    halves = [flat_sent[h * per_half : (h + 1) * per_half] for h in range(HALVES)]
+    halves = [flat[h * per_half : (h + 1) * per_half] for h in range(HALVES)]
 
     mine = [[half] + [lax.ppermute(half, "pool", shift(k)) for k in range(1, chips)] for half in halves]
     theirs = [[lax.ppermute(part, "pool", swap) for part in group] for group in mine]
 
     def places(h, every):
-        found = []
-        for core in (my_core, 1 - my_core):
-            for k in range(chips):
-                source = (my_chip - k + chips) % chips * 2 + core
-                found.append(
-                    lax.dynamic_slice(every, (source, h * per_half), (1, per_half))[0]
-                )
-        return jnp.broadcast_to(jnp.concatenate(found)[:, None], (pool_size * per_half, LANES))
+        found = every[:, h * per_half : (h + 1) * per_half].reshape(pool_size * per_half, 1)
+        return jnp.broadcast_to(found, (pool_size * per_half, LANES))
+
+    def code_sum(codes):
+        codes = codes.reshape(tp_size, -1, LANES)
+        turn = lambda k: [(i, (i + k) % tp_size) for i in range(tp_size)]
+        part = lambda index: lax.dynamic_index_in_dim(codes, index % tp_size, 0, False)
+        total = part(my_tp)
+        for k in range(1, tp_size):
+            total = total + lax.ppermute(part(my_tp + k), "tp", turn(k))
+        total = total.astype(jnp.bfloat16)
+        whole = jnp.zeros(codes.shape, jnp.bfloat16)
+        whole = lax.dynamic_update_index_in_dim(whole, total, my_tp, 0)
+        for k in range(1, tp_size):
+            other = lax.ppermute(total, "tp", turn(k))
+            whole = lax.dynamic_update_index_in_dim(
+                whole, other, (my_tp - k + tp_size) % tp_size, 0
+            )
+        return whole.reshape(-1, LANES)
 
     def partial_of(rows):
         return lax.dot_general(
@@ -182,15 +195,18 @@
         return lax.psum_scatter(partial, "tp", scatter_dimension=0, tiled=True)
 
     cut = lambda array, s: array[s * rows_count : (s + 1) * rows_count]
-    early = [partial_of(cut(flat, s)) for s in range(steps_count // HALVES)]
-    bases = [base_of(partial) for partial in early]
-    every, *_ = lax.optimization_barrier((every, *early))
+    first = steps_count // HALVES
+    groups = [cut(flat, s) for s in range(first)] + [flat[first * rows_count :]]
+    partials = [partial_of(rows) for rows in groups]
+    bases = [base_of(partial) for partial in partials]
+    every, *_ = lax.optimization_barrier((every, *partials))
     place = [places(h, every) for h in range(HALVES)]
     codes = [shrink(mine[h] + theirs[h], place[h], shrink_flat, rank) for h in range(HALVES)]
-    later, *codes = lax.optimization_barrier((flat[steps_count // HALVES * rows_count :], *codes))
-    partial, bases, codes = lax.optimization_barrier((partial_of(later), bases, codes))
-    codes = lax.psum(codes, "tp")
-    bases = [base.T for base in [*bases, base_of(partial)]]
+    codes = jnp.concatenate(codes, axis=0)
+    codes, bases[0] = lax.optimization_barrier((codes, bases[0]))
+    codes, *bases[1:first] = lax.optimization_barrier((code_sum(codes), *bases[1:first]))
+    codes = jnp.split(codes, HALVES, axis=0)
+    bases = [base.T for base in bases]
     moving = jnp.concatenate(bases, axis=0).astype(jnp.float32)
 
     updates = []

time: 250 us -> 253 us (1.012); the launches traced: 250 us -> 250 us
  starting transfers between devices: 7.03 us -> 19 us
  blocking collectives: 6.1 us -> 0 us
  waiting for transfers between devices: 128 us -> 125 us
    psum x1 -> x0, waiting for transfers between devices: 39.7 us -> none  [body(): codes = lax.psum(codes, 'tp')]
    ppermute x0 -> x8, waiting for transfers between devices: none -> 37.1 us  [the longest x3 24.9 us: code_sum(): total = total + lax.ppermute(part(my_tp + k), 'tp', turn(k))]
    ppermute x2, waiting for transfers between devices: 28.6 us -> 44.1 us  [body(): lax.ppermute(half, 'pool', shift(k))]
    reduce_scatter x3, waiting for transfers between devices: 14.8 us -> 0.06 us  [base_of(): return lax.psum_scatter(partial, 'tp', scatter_dimension=0, tiled=True)]
    ppermute x0 -> x8, starting transfers between devices: none -> 10.9 us  [the longest x3 5.18 us: code_sum(): total = total + lax.ppermute(part(my_tp + k), 'tp', turn(k))]
    all_gather x1 -> x0, blocking collectives: 6.1 us -> none  [body(): lax.all_gather(row_position.reshape(1, all_rows), 'pool', axis=0, tiled=T...]
  transfers between devices with their start and end apart: 16 -> 23, of which waited for: 7 -> 11; matrix products, arithmetic and copies ran while one was open for 16% -> 15% of each run, Pallas kernels for 12% -> 11%
where the time goes in v4:
time: 253 us; the launch traced here: 250 us
  waiting for transfers between devices  125 us (49%)
  matrix products  50.2 us (20%)
  Pallas kernels  28.5 us (11%)
  starting transfers between devices  19 us (8%)
  between operations  13.5 us (5%)
  local copies, waits for them, and re-layouts  8.84 us (3%)
  other arithmetic  4.55 us (2%)
    dot_general x3, matrix products, partial_of(): lax.dot_general(out_weight, rows, (((0,), (1,)), ((), ())), preferred_ele...  50.2 us
    ppermute x2, waiting for transfers between devices, body(): lax.ppermute(half, 'pool', shift(k))  44.1 us
    ppermute x2, waiting for transfers between devices, body(): joined = lax.ppermute(joined, 'pool', shift(chips - k))  44 us
    ppermute x3, waiting for transfers between devices, code_sum(): total = total + lax.ppermute(part(my_tp + k), 'tp', turn(k))  24.9 us
    pallas_call x2, Pallas kernels, shrink(): pl.pallas_call(functools.partial(shrink_kernel, count, rank), grid=(width...  16.9 us
    pallas_call x2, Pallas kernels, expand(): pl.pallas_call(functools.partial(expand_kernel, count, rank), grid=(featu...  11.6 us
    ppermute x3, waiting for transfers between devices, code_sum(): other = lax.ppermute(total, 'tp', turn(k))  9.26 us
    unnamed x23, local copies, waits for them, and re-layouts  6.63 us
  transfers between devices with their start and end apart: 23, of which 11 were waited for; matrix products, arithmetic and copies ran while one was open for 15% of the time, Pallas kernels for 11%

profile of v4, /device:TPU:0, one launch (start us, length us, event | category | flops | bytes accessed | tf_op | source)
XLA Modules:
  0.0 249.9 jit_solution(1834593697014269669)
XLA Ops:
  6.5 16.6 %convolution_convert_fusion.2 = bf16[8192,128]{0,1:T(8,128)(2,1)} fusion(bf16[2048,8192]{1,0:T(8,128)(2,1)} %param.8, bf16[4,128,2048]{2,1,0:T(8,128)(2,1)} %param.7), kind=kOutput, calls=%fused_computation.2 | convolution fusion | flops 4296015872 | bytes 36175872 | tf_op jit(solution)/shard_map/dot_general | solution.py:190
  23.2 17.0 %convolution_convert_fusion.1 = bf16[8192,128]{0,1:T(8,128)(2,1)} fusion(bf16[2048,8192]{1,0:T(8,128)(2,1)} %param.8, bf16[4,128,2048]{2,1,0:T(8,128)(2,1)} %param.7), kind=kOutput, calls=%fused_computation.1 | convolution fusion | flops 4296015872 | bytes 36175872 | tf_op jit(solution)/shard_map/dot_general | solution.py:190
  40.5 1.7 fusion.8
  42.2 16.6 %convolution_convert_fusion = bf16[8192,256]{0,1:T(8,128)(2,1)} fusion(bf16[256,2048]{1,0:T(8,128)(2,1)S(1)} %bitcast.54, bf16[2048,8192]{1,0:T(8,128)(2,1)} %param.8), kind=kOutput, calls=%fused_computation | convolution fusion | flops 8592031744 | bytes 38797312 | tf_op jit(solution)/shard_map/dot_general | solution.py:190
  58.8 3.0 %collective-permute-start.5 = (bf16[256,2048]{1,0:T(8,128)(2,1)S(1)}, bf16[256,2048]{1,0:T(8,128)(2,1)S(1)}, u32[]{:S(2)}, u32[]{:S(2)}) collective-permute-start(bf16[256,2048]{1,0:T(8,128)(2,1)S(1)} %bitcast.55), channel_id=1, source_target_pairs={{0,8},{4,12},{8,0},{12,4},{1,9},{5,13},{9,1},{13,5},{2,10},{6,14},... | collective-permute-start | bytes 3145736 | tf_op jit(solution)/shard_map/ppermute | solution.py:165
  61.9 23.9 %collective-permute-done.5.refs_1_ = bf16[256,2048]{1,0:T(8,128)(2,1)S(1)} collective-permute-done((bf16[256,2048]{1,0:T(8,128)(2,1)S(1)}, bf16[256,2048]{1,0:T(8,128)(2,1)S(1)}, u32[]{:S(2)}, u32[]{:S(2)}) %collective-permute-start.5) | collective-permute-done | bytes 1048608 | tf_op jit(solution)/shard_map/ppermute | solution.py:165
  85.9 1.0 copy-done.3
  87.4 20.2 %collective-permute-done.refs_1_ = bf16[256,2048]{1,0:T(8,128)(2,1)} collective-permute-done((bf16[256,2048]{1,0:T(8,128)(2,1)S(1)}, bf16[256,2048]{1,0:T(8,128)(2,1)}, u32[]{:S(2)}, u32[]{:S(2)}) %collective-permute-start) | collective-permute-done | bytes 1048608 | tf_op jit(solution)/shard_map/ppermute | solution.py:165
  107.9 1.8 collective-permute-start.3
  109.7 1.8 collective-permute-done.3
  111.6 1.1 collective-permute-done.4
  113.0 2.2 copy-done
  115.2 1.2 copy-done.4
  116.4 8.4 %shrink.3 = f32[512,128]{1,0:T(8,128)S(1)} custom-call(bf16[256,2048]{1,0:T(8,128)(2,1)S(1)} %bitcast.57, bf16[256,2048]{1,0:T(8,128)(2,1)S(1)} %copy-done.4, bf16[256,2048]{1,0:T(8,128)(2,1)} %collective-permute-done.6.refs_2_, bf16[256,2048]{1,0:T(8,128)(2,1)} %collective-permute-done.7.refs_3_, s32[1024,128]{1,0:T(8,128)S(1)} %broadcast_in_dim.61.refs_4_.place_ref, ...), custom_call_target="tpu_custom_call" | custom-call | flops 4294967296 | bytes 8388608 | tf_op jit(solution)/shard_map/shrink/pallas_call | solution.py:66
  125.0 8.5 %shrink.2 = f32[512,128]{1,0:T(8,128)S(1)} custom-call(bf16[256,2048]{1,0:T(8,128)(2,1)S(1)} %bitcast.53, bf16[256,2048]{1,0:T(8,128)(2,1)} %collective-permute-done.refs_1_, bf16[256,2048]{1,0:T(8,128)(2,1)} %collective-permute-done.1.refs_2_, bf16[256,2048]{1,0:T(8,128)(2,1)} %collective-permute-done.2.refs_3_, ...), custom_call_target="tpu_custom_call" | custom-call | flops 4294967296 | bytes 8388608 | tf_op jit(solution)/shard_map/shrink/pallas_call | solution.py:66
  133.7 4.0 %collective-permute-start.10 = (f32[256,128]{1,0:T(8,128)S(1)}, f32[256,128]{1,0:T(8,128)S(1)}, u32[]{:S(2)}, u32[]{:S(2)}) collective-permute-start(f32[256,128]{1,0:T(8,128)S(1)} %get-tuple-element.36), channel_id=1, source_target_pairs={{0,3},{1,0},{2,1},{3,2},{4,7},{5,4},{6,5},{7,6},{8,11},{9,8},{10,9... | collective-permute-start | bytes 393224 | tf_op jit(solution)/shard_map/ppermute | solution.py:178
  137.7 1.2 collective-permute-start.9
  138.9 7.6 %collective-permute-done.10 = f32[256,128]{1,0:T(8,128)S(1)} collective-permute-done((f32[256,128]{1,0:T(8,128)S(1)}, f32[256,128]{1,0:T(8,128)S(1)}, u32[]{:S(2)}, u32[]{:S(2)}) %collective-permute-start.10) | collective-permute-done | bytes 131104 | tf_op jit(solution)/shard_map/ppermute | solution.py:178
  146.5 4.5 %collective-permute-done.8 = f32[256,128]{1,0:T(8,128)S(1)} collective-permute-done((f32[256,128]{1,0:T(8,128)S(1)}, f32[256,128]{1,0:T(8,128)S(1)}, u32[]{:S(2)}, u32[]{:S(2)}) %collective-permute-start.8) | collective-permute-done | bytes 131104 | tf_op jit(solution)/shard_map/ppermute | solution.py:178
  151.0 12.7 %collective-permute-done.9 = f32[256,128]{1,0:T(8,128)S(1)} collective-permute-done((f32[256,128]{1,0:T(8,128)S(1)}, f32[256,128]{1,0:T(8,128)S(1)}, u32[]{:S(2)}, u32[]{:S(2)}) %collective-permute-start.9) | collective-permute-done | bytes 131104 | tf_op jit(solution)/shard_map/ppermute | solution.py:178
  163.9 3.3 %collective-permute-start.12 = (bf16[256,128]{1,0:T(8,128)(2,1)S(1)}, bf16[256,128]{1,0:T(8,128)(2,1)S(1)}, u32[]{:S(2)}, u32[]{:S(2)}) collective-permute-start(bf16[256,128]{1,0:T(8,128)(2,1)S(1)} %get-tuple-element.32), channel_id=1, source_target_pairs={{0,2},{1,3},{2,0},{3,1},{4,6},{5,7},{6,4},{7,5},{8,10},{9,11},{10,... | collective-permute-start | bytes 196616 | tf_op jit(solution)/shard_map/ppermute | solution.py:183
  167.7 4.4 %collective-permute-done.11 = bf16[256,128]{1,0:T(8,128)(2,1)S(1)} collective-permute-done((bf16[256,128]{1,0:T(8,128)(2,1)S(1)}, bf16[256,128]{1,0:T(8,128)(2,1)S(1)}, u32[]{:S(2)}, u32[]{:S(2)}) %collective-permute-start.11) | collective-permute-done | bytes 65568 | tf_op jit(solution)/shard_map/ppermute | solution.py:183
  172.2 4.8 %collective-permute-done.12 = bf16[256,128]{1,0:T(8,128)(2,1)S(1)} collective-permute-done((bf16[256,128]{1,0:T(8,128)(2,1)S(1)}, bf16[256,128]{1,0:T(8,128)(2,1)S(1)}, u32[]{:S(2)}, u32[]{:S(2)}) %collective-permute-start.12) | collective-permute-done | bytes 65568 | tf_op jit(solution)/shard_map/ppermute | solution.py:183
  177.1 2.2 copy-done.2
  179.3 5.8 %expand.2 = (bf16[256,2048]{1,0:T(8,128)(2,1)S(1)}, bf16[256,2048]{1,0:T(8,128)(2,1)S(1)}, bf16[256,2048]{1,0:T(8,128)(2,1)S(1)}, bf16[256,2048]{1,0:T(8,128)(2,1)S(1)}) custom-call(s32[1024,128]{1,0:T(8,128)S(1)} %broadcast_in_dim.59.refs_4_.place_ref, bf16[512,128]{1,0:T(8,128)(2,1)S(1)} %get-tuple-element.38.code_ref, bf16[1024,2048]{1,0:T(8,128)(2,1)S(1)} %bitcast.60), custom_call_target="tpu_custom_call" | custom-call | flops 4294967296 | bytes 8388608 | tf_op jit(solution)/shard_map/expand/pallas_call | solution.py:114
  185.2 5.8 %expand.3 = (bf16[256,2048]{1,0:T(8,128)(2,1)S(1)}, bf16[256,2048]{1,0:T(8,128)(2,1)S(1)}, bf16[256,2048]{1,0:T(8,128)(2,1)S(1)}, bf16[256,2048]{1,0:T(8,128)(2,1)S(1)}) custom-call(s32[1024,128]{1,0:T(8,128)S(1)} %broadcast_in_dim.61.refs_4_.place_ref, bf16[512,128]{1,0:T(8,128)(2,1)S(1)} %get-tuple-element.39.code_ref, bf16[1024,2048]{1,0:T(8,128)(2,1)S(1)} %bitcast.61), custom_call_target="tpu_custom_call" | custom-call | flops 4294967296 | bytes 8388608 | tf_op jit(solution)/shard_map/expand/pallas_call | solution.py:114
  191.0 0.6 collective-permute-start.18
  192.0 1.7 collective-permute-start.16
  194.3 1.7 collective-permute-start.19
  195.9 22.1 %collective-permute-done.16 = bf16[256,2048]{1,0:T(8,128)(2,1)S(1)} collective-permute-done((bf16[256,2048]{1,0:T(8,128)(2,1)S(1)}, bf16[256,2048]{1,0:T(8,128)(2,1)S(1)}, u32[]{:S(2)}, u32[]{:S(2)}) %collective-permute-start.16) | collective-permute-done | bytes 1048608 | tf_op jit(solution)/shard_map/ppermute | solution.py:219
  218.2 21.8 %collective-permute-done.19 = bf16[256,2048]{1,0:T(8,128)(2,1)S(1)} collective-permute-done((bf16[256,2048]{1,0:T(8,128)(2,1)S(1)}, bf16[256,2048]{1,0:T(8,128)(2,1)S(1)}, u32[]{:S(2)}, u32[]{:S(2)}) %collective-permute-start.19) | collective-permute-done | bytes 1048608 | tf_op jit(solution)/shard_map/ppermute | solution.py:219
  240.3 3.1 %add_convert_fusion = bf16[512,2048]{1,0:T(8,128)(2,1)} fusion(bf16[256,2048]{1,0:T(8,128)(2,1)} %bitcast.65, bf16[128,2048]{1,0:T(8,128)(2,1)S(1)} %bitcast.67, bf16[128,2048]{1,0:T(8,128)(2,1)S(1)} %bitcast.66, bf16[256,2048]{1,0:T(8,128)(2,1)S(1)} %add_add_fusion, bf16[256,2048]{1,0:T(8,128)(2,1)S(1)} %add_add_fusion.1), kind=kLoop, calls=%fused_computation.3 | loop fusion | flops 13631488 | bytes 6291456 | tf_op jit(solution)/shard_map/convert_element_type | solution.py:224
  (67 shorter events, 4.0 us)
Async XLA Ops:
  6.5 127.1 %reduce-scatter.4.cloned.1.call-start = ((), (), s32[]{:S(2)}) async-start(), calls=%async_computation.3 | async-start | bytes 2621440 | tf_op jit(solution)/shard_map/reduce_scatter | solution.py:195
  23.2 153.9 %reduce-scatter.6.cloned.1.call-start = ((), (), s32[]{:S(2)}) async-start(), calls=%async_computation.4 | async-start | bytes 2621440 | tf_op jit(solution)/shard_map/reduce_scatter | solution.py:195
  40.2 200.0 %reduce-scatter.8.cloned.1.call-start = ((), (), s32[]{:S(2)}) async-start(), calls=%async_computation.5 | async-start | bytes 5242880 | tf_op jit(solution)/shard_map/reduce_scatter | solution.py:195
  58.8 48.8 %copy-start.8 = (s32[4,1,8]{2,1,0:T(1,128)S(1)}, s32[4,1,8]{2,1,0:T(1,128)}, u32[]{:S(2)}) copy-start(s32[4,1,8]{2,1,0:T(1,128)} %param.12) | copy-start | bytes 388
  58.8 48.8 %copy-start.9 = (s32[64]{0:T(128)S(1)}, s32[64]{0:T(128)}, u32[]{:S(2)}) copy-start(s32[64]{0:T(128)} %param.11) | copy-start | bytes 772
  58.8 49.0 %copy-start.7 = (s32[4,128]{1,0:T(4,128)S(1)}, s32[4,128]{1,0:T(4,128)}, u32[]{:S(2)}) copy-start(s32[4,128]{1,0:T(4,128)} %param.13) | copy-start | bytes 6148
  58.8 27.0 %collective-permute-start.5 = (bf16[256,2048]{1,0:T(8,128)(2,1)S(1)}, bf16[256,2048]{1,0:T(8,128)(2,1)S(1)}, u32[]{:S(2)}, u32[]{:S(2)}) collective-permute-start(bf16[256,2048]{1,0:T(8,128)(2,1)S(1)} %bitcast.55), channel_id=1, source_target_pairs={{0,8},{4,12},{8,0},{12,4},{1,9},{5,13},{9,1},{13,5},{2,10},{6,14},... | collective-permute-start | bytes 3145736 | tf_op jit(solution)/shard_map/ppermute | solution.py:165
  61.9 45.7 %collective-permute-start = (bf16[256,2048]{1,0:T(8,128)(2,1)S(1)}, bf16[256,2048]{1,0:T(8,128)(2,1)}, u32[]{:S(2)}, u32[]{:S(2)}) collective-permute-start(bf16[256,2048]{1,0:T(8,128)(2,1)S(1)} %bitcast.51), channel_id=1, source_target_pairs={{0,8},{4,12},{8,0},{12,4},{1,9},{5,13},{9,1},{13,5},{2,10},{6,14},... | collective-permute-start | bytes 3145736 | tf_op jit(solution)/shard_map/ppermute | solution.py:165
  61.9 50.8 %collective-permute-start.6 = (bf16[256,2048]{1,0:T(8,128)(2,1)S(1)}, bf16[256,2048]{1,0:T(8,128)(2,1)}, u32[]{:S(2)}, u32[]{:S(2)}) collective-permute-start(bf16[256,2048]{1,0:T(8,128)(2,1)S(1)} %bitcast.56), channel_id=1, source_target_pairs={{0,4},{4,0},{8,12},{12,8},{1,5},{5,1},{9,13},{13,9},{2,6},{6,2},{1... | collective-permute-start | bytes 3145736 | tf_op jit(solution)/shard_map/ppermute | solution.py:166
  85.9 26.9 %collective-permute-start.7 = (bf16[256,2048]{1,0:T(8,128)(2,1)S(1)}, bf16[256,2048]{1,0:T(8,128)(2,1)}, u32[]{:S(2)}, u32[]{:S(2)}) collective-permute-start(bf16[256,2048]{1,0:T(8,128)(2,1)S(1)} %collective-permute-done.5.refs_1_), channel_id=1, source_target_pairs={{0,4},{4,0},{8,12},{12,8},{1,5},{5,1},{9,13},{13,9},{2,6},{6,2},{1... | collective-permute-start | bytes 3145736 | tf_op jit(solution)/shard_map/ppermute | solution.py:166
  86.9 37.9 %collective-permute-start.1 = (bf16[256,2048]{1,0:T(8,128)(2,1)S(1)}, bf16[256,2048]{1,0:T(8,128)(2,1)}, u32[]{:S(2)}, u32[]{:S(2)}) collective-permute-start(bf16[256,2048]{1,0:T(8,128)(2,1)S(1)} %bitcast.52), channel_id=1, source_target_pairs={{0,4},{4,0},{8,12},{12,8},{1,5},{5,1},{9,13},{13,9},{2,6},{6,2},{1... | collective-permute-start | bytes 3145736 | tf_op jit(solution)/shard_map/ppermute | solution.py:166
  107.6 17.2 %collective-permute-start.2 = (bf16[256,2048]{1,0:T(8,128)(2,1)}, bf16[256,2048]{1,0:T(8,128)(2,1)}, u32[]{:S(2)}, u32[]{:S(2)}) collective-permute-start(bf16[256,2048]{1,0:T(8,128)(2,1)} %collective-permute-done.refs_1_), channel_id=1, source_target_pairs={{0,4},{4,0},{8,12},{12,8},{1,5},{5,1},{9,13},{13,9},{2,6},{6,2},{1... | collective-permute-start | bytes 3145736 | tf_op jit(solution)/shard_map/ppermute | solution.py:166
  107.9 3.6 %collective-permute-start.3 = (s32[1,512]{1,0:T(1,128)S(1)}, s32[1,512]{1,0:T(1,128)S(1)}, u32[]{:S(2)}, u32[]{:S(2)}) collective-permute-start(s32[1,512]{1,0:T(1,128)S(1)} %bitcast.68), channel_id=1, source_target_pairs={{0,8},{4,12},{8,0},{12,4},{1,9},{5,13},{9,1},{13,5},{2,10},{6,14},... | collective-permute-start | bytes 6152 | tf_op jit(solution)/shard_map/ppermute | solution.py:157
  111.5 1.2 collective-permute-start.4
  113.0 2.2 copy-start
  115.2 1.2 copy-start.4
  116.4 8.6 %copy-start.1 = (bf16[16,64,2048]{2,1,0:T(8,128)(2,1)S(1)}, bf16[16,64,2048]{2,1,0:T(8,128)(2,1)}, u32[]{:S(2)}) copy-start(bf16[16,64,2048]{2,1,0:T(8,128)(2,1)} %param.9) | copy-start | bytes 12582916
  133.7 12.8 %collective-permute-start.10 = (f32[256,128]{1,0:T(8,128)S(1)}, f32[256,128]{1,0:T(8,128)S(1)}, u32[]{:S(2)}, u32[]{:S(2)}) collective-permute-start(f32[256,128]{1,0:T(8,128)S(1)} %get-tuple-element.36), channel_id=1, source_target_pairs={{0,3},{1,0},{2,1},{3,2},{4,7},{5,4},{6,5},{7,6},{8,11},{9,8},{10,9... | collective-permute-start | bytes 393224 | tf_op jit(solution)/shard_map/ppermute | solution.py:178
  137.7 13.3 %collective-permute-start.8 = (f32[256,128]{1,0:T(8,128)S(1)}, f32[256,128]{1,0:T(8,128)S(1)}, u32[]{:S(2)}, u32[]{:S(2)}) collective-permute-start(f32[256,128]{1,0:T(8,128)S(1)} %get-tuple-element.35), channel_id=1, source_target_pairs={{0,1},{1,2},{2,3},{3,0},{4,5},{5,6},{6,7},{7,4},{8,9},{9,10},{10,1... | collective-permute-start | bytes 393224 | tf_op jit(solution)/shard_map/ppermute | solution.py:178
  137.7 26.0 %collective-permute-start.9 = (f32[256,128]{1,0:T(8,128)S(1)}, f32[256,128]{1,0:T(8,128)S(1)}, u32[]{:S(2)}, u32[]{:S(2)}) collective-permute-start(f32[256,128]{1,0:T(8,128)S(1)} %get-tuple-element.37), channel_id=1, source_target_pairs={{0,2},{1,3},{2,0},{3,1},{4,6},{5,7},{6,4},{7,5},{8,10},{9,11},{10,... | collective-permute-start | bytes 393224 | tf_op jit(solution)/shard_map/ppermute | solution.py:178
  163.8 8.3 %collective-permute-start.11 = (bf16[256,128]{1,0:T(8,128)(2,1)S(1)}, bf16[256,128]{1,0:T(8,128)(2,1)S(1)}, u32[]{:S(2)}, u32[]{:S(2)}) collective-permute-start(bf16[256,128]{1,0:T(8,128)(2,1)S(1)} %get-tuple-element.32), channel_id=1, source_target_pairs={{0,1},{1,2},{2,3},{3,0},{4,5},{5,6},{6,7},{7,4},{8,9},{9,10},{10,1... | collective-permute-start | bytes 196616 | tf_op jit(solution)/shard_map/ppermute | solution.py:183
  163.9 13.1 %collective-permute-start.12 = (bf16[256,128]{1,0:T(8,128)(2,1)S(1)}, bf16[256,128]{1,0:T(8,128)(2,1)S(1)}, u32[]{:S(2)}, u32[]{:S(2)}) collective-permute-start(bf16[256,128]{1,0:T(8,128)(2,1)S(1)} %get-tuple-element.32), channel_id=1, source_target_pairs={{0,2},{1,3},{2,0},{3,1},{4,6},{5,7},{6,4},{7,5},{8,10},{9,11},{10,... | collective-permute-start | bytes 196616 | tf_op jit(solution)/shard_map/ppermute | solution.py:183
  167.2 9.8 %collective-permute-start.13 = (bf16[256,128]{1,0:T(8,128)(2,1)S(1)}, bf16[256,128]{1,0:T(8,128)(2,1)S(1)}, u32[]{:S(2)}, u32[]{:S(2)}) collective-permute-start(bf16[256,128]{1,0:T(8,128)(2,1)S(1)} %get-tuple-element.32), channel_id=1, source_target_pairs={{0,3},{1,0},{2,1},{3,2},{4,7},{5,4},{6,5},{7,6},{8,11},{9,8},{10,9... | collective-permute-start | bytes 196616 | tf_op jit(solution)/shard_map/ppermute | solution.py:183
  177.1 2.2 copy-start.2
  185.1 6.5 %collective-permute-start.15 = (bf16[256,2048]{1,0:T(8,128)(2,1)S(1)}, bf16[256,2048]{1,0:T(8,128)(2,1)S(1)}, u32[]{:S(2)}, u32[]{:S(2)}) collective-permute-start(bf16[256,2048]{1,0:T(8,128)(2,1)S(1)} %get-tuple-element.26), channel_id=1, source_target_pairs={{0,4},{4,0},{8,12},{12,8},{1,5},{5,1},{9,13},{13,9},{2,6},{6,2},{1... | collective-permute-start | bytes 3145736 | tf_op jit(solution)/shard_map/ppermute | solution.py:217
  191.0 2.9 %collective-permute-start.18 = (bf16[256,2048]{1,0:T(8,128)(2,1)S(1)}, bf16[256,2048]{1,0:T(8,128)(2,1)S(1)}, u32[]{:S(2)}, u32[]{:S(2)}) collective-permute-start(bf16[256,2048]{1,0:T(8,128)(2,1)S(1)} %get-tuple-element.30), channel_id=1, source_target_pairs={{0,4},{4,0},{8,12},{12,8},{1,5},{5,1},{9,13},{13,9},{2,6},{6,2},{1... | collective-permute-start | bytes 3145736 | tf_op jit(solution)/shard_map/ppermute | solution.py:217
  191.5 4.4 %collective-permute-start.14 = (bf16[256,2048]{1,0:T(8,128)(2,1)S(1)}, bf16[256,2048]{1,0:T(8,128)(2,1)S(1)}, u32[]{:S(2)}, u32[]{:S(2)}) collective-permute-start(bf16[256,2048]{1,0:T(8,128)(2,1)S(1)} %get-tuple-element.24), channel_id=1, source_target_pairs={{0,4},{4,0},{8,12},{12,8},{1,5},{5,1},{9,13},{13,9},{2,6},{6,2},{1... | collective-permute-start | bytes 3145736 | tf_op jit(solution)/shard_map/ppermute | solution.py:217
  192.0 26.0 %collective-permute-start.16 = (bf16[256,2048]{1,0:T(8,128)(2,1)S(1)}, bf16[256,2048]{1,0:T(8,128)(2,1)S(1)}, u32[]{:S(2)}, u32[]{:S(2)}) collective-permute-start(bf16[256,2048]{1,0:T(8,128)(2,1)S(1)} %add.111), channel_id=1, source_target_pairs={{0,8},{4,12},{8,0},{12,4},{1,9},{5,13},{9,1},{13,5},{2,10},{6,14},... | collective-permute-start | bytes 3145736 | tf_op jit(solution)/shard_map/ppermute | solution.py:219
  193.7 24.5 %collective-permute-start.17 = (bf16[256,2048]{1,0:T(8,128)(2,1)S(1)}, bf16[256,2048]{1,0:T(8,128)(2,1)S(1)}, u32[]{:S(2)}, u32[]{:S(2)}) collective-permute-start(bf16[256,2048]{1,0:T(8,128)(2,1)S(1)} %get-tuple-element.28), channel_id=1, source_target_pairs={{0,4},{4,0},{8,12},{12,8},{1,5},{5,1},{9,13},{13,9},{2,6},{6,2},{1... | collective-permute-start | bytes 3145736 | tf_op jit(solution)/shard_map/ppermute | solution.py:217
  194.3 45.8 %collective-permute-start.19 = (bf16[256,2048]{1,0:T(8,128)(2,1)S(1)}, bf16[256,2048]{1,0:T(8,128)(2,1)S(1)}, u32[]{:S(2)}, u32[]{:S(2)}) collective-permute-start(bf16[256,2048]{1,0:T(8,128)(2,1)S(1)} %add.114), channel_id=1, source_target_pairs={{0,8},{4,12},{8,0},{12,4},{1,9},{5,13},{9,1},{13,5},{2,10},{6,14},... | collective-permute-start | bytes 3145736 | tf_op jit(solution)/shard_map/ppermute | solution.py:219
  218.0 22.2 %copy-start.5 = (bf16[2048,128]{0,1:T(8,128)(2,1)S(1)}, bf16[2048,128]{0,1:T(8,128)(2,1)}, u32[]{:S(2)}) copy-start(bf16[2048,128]{0,1:T(8,128)(2,1)} %reduce-scatter.4.cloned.1.call-done) | copy-start | bytes 1572868
  218.0 22.2 %copy-start.6 = (bf16[2048,128]{0,1:T(8,128)(2,1)S(1)}, bf16[2048,128]{0,1:T(8,128)(2,1)}, u32[]{:S(2)}) copy-start(bf16[2048,128]{0,1:T(8,128)(2,1)} %reduce-scatter.6.cloned.1.call-done) | copy-start | bytes 1572868
  (1 other events, 1.0 us)
Sparse Core Ops, SparseCore 0:
  23.3 46.5 reduce-scatter.3
  72.3 43.1 reduce-scatter.5
  117.8 88.6 reduce-scatter.7
